TPU v7x, 32 devices: a whole 2x2x4 slice. The times are simulated.
32 devices in a mesh: seq: 4 (over y, core), fsdp: 8 (over z, x).
Axes of the slice: x: 2, y: 2, z: 4, core: 2. Of those that a mesh axis runs over, the one named last changes fastest.
Arguments:
- inputs: bfloat16 [8, 2048, 768], P('fsdp', 'seq'), may hold values from -6 to 6
- norm_one: bfloat16 [768], P('fsdp'), may hold values from 0.5 to 1.5
- qkv_weight: bfloat16 [768, 2304], P('fsdp'), may hold values from -0.21875 to 0.21875
- attn_out_weight: bfloat16 [768, 768], P('fsdp'), may hold values from -6 to 6
- norm_two: bfloat16 [768], P('fsdp'), may hold values from 0.5 to 1.5
- mlp_in_weight: bfloat16 [768, 2304], P('fsdp'), may hold values from -0.21875 to 0.21875
- mlp_out_weight: bfloat16 [1152, 768], P('fsdp'), may hold values from -0.1875 to 0.1875
- cotangent: bfloat16 [8, 2048, 768], P('fsdp', 'seq'), may hold values from -6 to 6
Outputs:
- output: bfloat16 [8, 2048, 768], P('fsdp', 'seq')
- input_grad: bfloat16 [8, 2048, 768], P('fsdp', 'seq')
- norm_one_grad: float32 [768], P('fsdp')
- qkv_grad: float32 [768, 2304], P('fsdp')
- attn_out_grad: float32 [768, 768], P('fsdp')
- norm_two_grad: float32 [768], P('fsdp')
- mlp_in_grad: float32 [768, 2304], P('fsdp')
- mlp_out_grad: float32 [1152, 768], P('fsdp')
All inputs are finite; a program needn't handle non-finite values.
Results may differ from a plain program's by a relative error of at most 0.018.
Values may be sent and summed in bfloat16 or wider, within the bound.
No kernel may reach another device: no remote copies, remote signals or barrier semaphores. Data moves between devices by JAX's collectives and lax.ppermute only.
A program may use at most 128 MiB of HBM per device.

v0:
```python
import jax
import jax.numpy as jnp
from jax import lax
from jax.sharding import PartitionSpec as P

HEADS = 12
HEAD = 64


EPSILON = 1e-05
ROPE_BASE = 160000.0


def matmul(left, right):
    return jnp.dot(left, right, preferred_element_type=jnp.float32)


def left_contract(left, right):
    return lax.dot_general(
        left, right, (((0,), (0,)), ((), ())), preferred_element_type=jnp.float32
    )


def right_contract(left, right):
    return lax.dot_general(
        left, right, (((1,), (1,)), ((), ())), preferred_element_type=jnp.float32
    )


def normalize(values):
    centred = values - jnp.mean(values, axis=1, keepdims=True)
    variance = jnp.mean(centred * centred, axis=1, keepdims=True)
    scale_inv = lax.rsqrt(variance + EPSILON)
    return (centred * scale_inv, scale_inv)


def norm_back(grad_hat, normed, scale_inv):
    return scale_inv * (
        grad_hat
        - jnp.mean(grad_hat, axis=1, keepdims=True)
        - normed * jnp.mean(grad_hat * normed, axis=1, keepdims=True)
    )


def rope_tables(offset, count, head_size):
    half_size = head_size // 2
    places = offset.astype(jnp.float32) + jnp.arange(count, dtype=jnp.float32)
    inverse = ROPE_BASE ** (-(jnp.arange(half_size, dtype=jnp.float32) * 2.0 / head_size))
    angles = places[:, None] * inverse[None, :]
    angles = jnp.concatenate([angles, angles], axis=1)
    return (jnp.cos(angles), jnp.sin(angles))


def rotate(values, cosine, sine, head_size):
    half_size = head_size // 2
    shaped = values.reshape(values.shape[0], -1, head_size)
    turned = jnp.concatenate([-shaped[..., half_size:], shaped[..., :half_size]], axis=-1)
    return (shaped * cosine[:, None, :] + turned * sine[:, None, :]).reshape(values.shape)


def rotate_back(grads, cosine, sine, head_size):
    half_size = head_size // 2
    shaped = grads.reshape(grads.shape[0], -1, head_size)
    scaled = shaped * sine[:, None, :]
    turned = jnp.concatenate([scaled[..., half_size:], -scaled[..., :half_size]], axis=-1)
    return (shaped * cosine[:, None, :] + turned).reshape(grads.shape)


def attend_forward(queries, keys, values, heads_here, head_size, block):
    length = queries.shape[0]
    count = length // block
    scale = head_size ** (-0.5)
    key_heads = keys.reshape(length, heads_here, head_size)
    value_heads = values.reshape(length, heads_here, head_size)
    query_blocks = queries.reshape(count, block, heads_here, head_size)

    def one_block(query_block):
        scores = (
            jnp.einsum("qhd,khd->hqk", query_block, key_heads, preferred_element_type=jnp.float32)
            * scale
        )
        top = jnp.max(scores, axis=2, keepdims=True)
        weights = jnp.exp(scores - top)
        totals = jnp.sum(weights, axis=2, keepdims=True)
        probs = (weights / totals).astype(jnp.bfloat16)
        context = jnp.einsum("hqk,khd->qhd", probs, value_heads, preferred_element_type=jnp.float32)
        return (
            context.astype(jnp.bfloat16).reshape(block, heads_here * head_size),
            (top + jnp.log(totals))[..., 0],
        )

    contexts, log_sums = lax.map(one_block, query_blocks)
    return (contexts.reshape(length, heads_here * head_size), log_sums)


def attend_backward(queries, keys, values, grad_context, log_sums, heads_here, head_size, block):
    length = queries.shape[0]
    count = length // block
    scale = head_size ** (-0.5)
    key_heads = keys.reshape(length, heads_here, head_size)
    value_heads = values.reshape(length, heads_here, head_size)
    query_blocks = queries.reshape(count, block, heads_here, head_size)
    grad_blocks = grad_context.reshape(count, block, heads_here, head_size)

    def one_block(carry, pieces):
        key_grad, value_grad = carry
        query_block, grad_block, log_block = pieces
        scores = (
            jnp.einsum("qhd,khd->hqk", query_block, key_heads, preferred_element_type=jnp.float32)
            * scale
        )
        probs = jnp.exp(scores - log_block[..., None])
        probs_low = probs.astype(jnp.bfloat16)
        prob_grad = jnp.einsum(
            "qhd,khd->hqk", grad_block, value_heads, preferred_element_type=jnp.float32
        )
        centre = jnp.sum(probs * prob_grad, axis=2, keepdims=True)
        score_grad = (probs * (prob_grad - centre)).astype(jnp.bfloat16)
        query_grad = (
            jnp.einsum("hqk,khd->qhd", score_grad, key_heads, preferred_element_type=jnp.float32)
            * scale
        )
        key_grad = (
            key_grad
            + jnp.einsum(
                "hqk,qhd->khd", score_grad, query_block, preferred_element_type=jnp.float32
            )
            * scale
        )
        value_grad = value_grad + jnp.einsum(
            "hqk,qhd->khd", probs_low, grad_block, preferred_element_type=jnp.float32
        )
        return (
            (key_grad, value_grad),
            query_grad.astype(jnp.bfloat16).reshape(block, heads_here * head_size),
        )

    zeros = jnp.zeros((length, heads_here, head_size), jnp.float32)
    (key_grad, value_grad), query_grads = lax.scan(
        one_block, (zeros, zeros), (query_blocks, grad_blocks, log_sums)
    )
    width = heads_here * head_size
    return (
        query_grads.reshape(length, width),
        key_grad.reshape(length, width).astype(jnp.bfloat16),
        value_grad.reshape(length, width).astype(jnp.bfloat16),
    )


def body(
    inputs,
    norm_one,
    qkv_weight,
    attn_out_weight,
    norm_two,
    mlp_in_weight,
    mlp_out_weight,
    cotangent,
):
    gathered = (
        lax.all_gather(norm_one, "fsdp", axis=0, tiled=True),
        lax.all_gather(qkv_weight, "fsdp", axis=0, tiled=True),
        lax.all_gather(attn_out_weight, "fsdp", axis=0, tiled=True),
        lax.all_gather(norm_two, "fsdp", axis=0, tiled=True),
        lax.all_gather(mlp_in_weight, "fsdp", axis=0, tiled=True),
        lax.all_gather(mlp_out_weight, "fsdp", axis=0, tiled=True),
    )
    gain_one, w_qkv, w_attn, gain_two, w_in, w_out = gathered
    width = w_attn.shape[0]
    hidden_size = w_out.shape[0]
    slices = lax.axis_size("seq")
    heads_here = HEADS // slices
    rows = inputs.shape[1]
    length = rows * slices
    block = min(512, length)
    cosine, sine = rope_tables(lax.axis_index("seq") * rows, rows, HEAD)
    float_input = inputs[0].astype(jnp.float32)
    normed_hat1, scale_one = normalize(float_input)
    normed_low1 = (normed_hat1 * gain_one.astype(jnp.float32)).astype(jnp.bfloat16)
    qkv = matmul(normed_low1, w_qkv)
    query_low = rotate(qkv[:, :width], cosine, sine, HEAD).astype(jnp.bfloat16)
    key_low = rotate(qkv[:, width : 2 * width], cosine, sine, HEAD).astype(jnp.bfloat16)
    value_low = qkv[:, 2 * width :].astype(jnp.bfloat16)
    query_all, key_all, value_all = (
        lax.all_to_all(query_low, "seq", split_axis=1, concat_axis=0, tiled=True),
        lax.all_to_all(key_low, "seq", split_axis=1, concat_axis=0, tiled=True),
        lax.all_to_all(value_low, "seq", split_axis=1, concat_axis=0, tiled=True),
    )
    context_all, log_sums = attend_forward(query_all, key_all, value_all, heads_here, HEAD, block)
    context_low = lax.all_to_all(context_all, "seq", split_axis=0, concat_axis=1, tiled=True)
    attended = float_input + matmul(context_low, w_attn)
    normed_hat2, scale_two = normalize(attended)
    normed_low2 = (normed_hat2 * gain_two.astype(jnp.float32)).astype(jnp.bfloat16)
    gate_up = matmul(normed_low2, w_in)
    first_half = gate_up[:, :hidden_size]
    second_half = gate_up[:, hidden_size:]
    gelu_first, gelu_back = jax.vjp(lambda entry: jax.nn.gelu(entry, approximate=False), first_half)
    hidden_low = (gelu_first * second_half).astype(jnp.bfloat16)
    result = (attended + matmul(hidden_low, w_out)).astype(jnp.bfloat16)
    regathered = (
        lax.all_gather(norm_one, "fsdp", axis=0, tiled=True),
        lax.all_gather(qkv_weight, "fsdp", axis=0, tiled=True),
        lax.all_gather(attn_out_weight, "fsdp", axis=0, tiled=True),
        lax.all_gather(norm_two, "fsdp", axis=0, tiled=True),
        lax.all_gather(mlp_in_weight, "fsdp", axis=0, tiled=True),
        lax.all_gather(mlp_out_weight, "fsdp", axis=0, tiled=True),
    )
    back_gain1, back_qkv, back_attn, back_gain2, back_in, back_out = regathered
    grad_low = cotangent[0]
    grad_w_out = left_contract(hidden_low, grad_low)
    hidden_grad = right_contract(grad_low, back_out)
    first_grad = gelu_back(hidden_grad * second_half)[0]
    second_grad = hidden_grad * gelu_first
    gate_up_grad = jnp.concatenate([first_grad, second_grad], axis=1).astype(jnp.bfloat16)
    grad_w_in = left_contract(normed_low2, gate_up_grad)
    normed_grad2 = right_contract(gate_up_grad, back_in)
    grad_gain2 = jnp.sum(normed_grad2 * normed_hat2, axis=0)
    attended_grad = grad_low.astype(jnp.float32) + norm_back(
        normed_grad2 * back_gain2.astype(jnp.float32), normed_hat2, scale_two
    )
    branch_low = attended_grad.astype(jnp.bfloat16)
    grad_w_attn = left_contract(context_low, branch_low)
    context_grad = right_contract(branch_low, back_attn).astype(jnp.bfloat16)
    context_grad_all = lax.all_to_all(context_grad, "seq", split_axis=1, concat_axis=0, tiled=True)
    query_grad_all, key_grad_all, value_grad_all = attend_backward(
        query_all, key_all, value_all, context_grad_all, log_sums, heads_here, HEAD, block
    )
    query_grad, key_grad, value_grad = (
        lax.all_to_all(query_grad_all, "seq", split_axis=0, concat_axis=1, tiled=True),
        lax.all_to_all(key_grad_all, "seq", split_axis=0, concat_axis=1, tiled=True),
        lax.all_to_all(value_grad_all, "seq", split_axis=0, concat_axis=1, tiled=True),
    )
    query_turned = rotate_back(query_grad.astype(jnp.float32), cosine, sine, HEAD).astype(
        jnp.bfloat16
    )
    key_turned = rotate_back(key_grad.astype(jnp.float32), cosine, sine, HEAD).astype(jnp.bfloat16)
    qkv_grad_low = jnp.concatenate([query_turned, key_turned, value_grad], axis=1)
    grad_w_qkv = left_contract(normed_low1, qkv_grad_low)
    normed_grad1 = right_contract(qkv_grad_low, back_qkv)
    grad_gain1 = jnp.sum(normed_grad1 * normed_hat1, axis=0)
    input_grad = attended_grad + norm_back(
        normed_grad1 * back_gain1.astype(jnp.float32), normed_hat1, scale_one
    )
    owned = (
        lax.psum_scatter(grad_gain1, "fsdp", scatter_dimension=0, tiled=True),
        lax.psum_scatter(grad_w_qkv, "fsdp", scatter_dimension=0, tiled=True),
        lax.psum_scatter(grad_w_attn, "fsdp", scatter_dimension=0, tiled=True),
        lax.psum_scatter(grad_gain2, "fsdp", scatter_dimension=0, tiled=True),
        lax.psum_scatter(grad_w_in, "fsdp", scatter_dimension=0, tiled=True),
        lax.psum_scatter(grad_w_out, "fsdp", scatter_dimension=0, tiled=True),
    )
    totals = (
        lax.psum(owned[0].astype(jnp.bfloat16), "seq").astype(jnp.float32),
        lax.psum(owned[1].astype(jnp.bfloat16), "seq").astype(jnp.float32),
        lax.psum(owned[2].astype(jnp.bfloat16), "seq").astype(jnp.float32),
        lax.psum(owned[3].astype(jnp.bfloat16), "seq").astype(jnp.float32),
        lax.psum(owned[4].astype(jnp.bfloat16), "seq").astype(jnp.float32),
        lax.psum(owned[5].astype(jnp.bfloat16), "seq").astype(jnp.float32),
    )
    return (
        result[None],
        input_grad.astype(jnp.bfloat16)[None],
        totals[0],
        totals[1],
        totals[2],
        totals[3],
        totals[4],
        totals[5],
    )


def solution(mesh):
    placed = (
        P("fsdp", "seq", None),
        P("fsdp"),
        P("fsdp", None),
        P("fsdp", None),
        P("fsdp"),
        P("fsdp", None),
        P("fsdp", None),
        P("fsdp", "seq", None),
    )
    return jax.shard_map(
        body,
        mesh=mesh,
        in_specs=placed,
        out_specs=(
            P("fsdp", "seq", None),
            P("fsdp", "seq", None),
            P("fsdp"),
            P("fsdp", None),
            P("fsdp", None),
            P("fsdp"),
            P("fsdp", None),
            P("fsdp", None),
        ),
        check_vma=False,
    )
```

profile of v0, /device:TPU:1, one launch (start us, length us, event | category | flops | bytes accessed | tf_op | source)
XLA Modules:
  0.0 720.0 jit_solution(6701847524023451738)
XLA Ops:
  13.1 19.1 %all-reduce.5 = (bf16[768]{0:T(1024)(128)(2,1)S(1)}, bf16[768]{0:T(1024)(128)(2,1)S(1)}) all-reduce(bf16[768]{0:T(1024)(128)(2,1)S(1)} %dynamic-update-slice, bf16[768]{0:T(1024)(128)(2,1)S(1)} %dynamic-update-slice.1), channel_id=1, replica_groups=mesh['seq'=4,'fsdp'=8] {'fsdp'}, use_global_device_ids=true, to_apply=%add | all-reduce | flops 1536 | bytes 6144
  36.4 40.3 %all-gather.5.cloned.1.call-done = bf16[768,2304]{1,0:T(8,128)(2,1)} async-done(((bf16[96,2304]{1,0:T(8,128)(2,1)}), bf16[768,2304]{1,0:T(8,128)(2,1)}) %all-gather.5.cloned.1.call-update) | async-done | bytes 3538960 | tf_op jit(solution)/shard_map/all_gather | solution.py:162
  76.7 4.1 fusion.84
  84.0 3.0 copy.54
  87.0 3.1 copy.50
  94.8 3.0 copy.51
  97.8 3.1 copy.55
  100.9 4.2 add_convert_fusion.2
  107.4 5.3 all-to-all-start.1
  115.4 8.1 %all-to-all-done.1 = bf16[512,4,192]{0,2,1:T(8,128)(2,1)S(1)} async-done(((bf16[512,4,192]{0,2,1:T(8,128)(2,1)}), bf16[512,4,192]{0,2,1:T(8,128)(2,1)S(1)}, u32[]{:S(2)}, u32[]{:S(2)}) %all-to-all-start.1) | async-done | bytes 786464 | tf_op jit(solution)/shard_map/all_to_all | solution.py:186
  123.5 4.3 all-to-all-start.2
  129.0 9.7 %all-to-all-done.2 = bf16[512,4,192]{0,2,1:T(8,128)(2,1)S(1)} async-done(((bf16[512,4,192]{0,2,1:T(8,128)(2,1)}), bf16[512,4,192]{0,2,1:T(8,128)(2,1)S(1)}, u32[]{:S(2)}, u32[]{:S(2)}) %all-to-all-start.2) | async-done | bytes 786464 | tf_op jit(solution)/shard_map/all_to_all | solution.py:187
  138.7 4.2 all-to-all-start
  150.7 3.0 all-to-all-done
  154.7 34.0 %while.27 = (s32[]{:T(128)}, bf16[4,512,192]{1,2,0:T(8,128)(2,1)}, f32[4,3,512]{2,1,0:T(4,128)S(1)}, bf16[4,512,3,64]{1,3,2,0:T(8,128)(2,1)S(1)}, bf16[2048,3,64...) while((s32[]{:T(128)}, bf16[4,512,192]{1,2,0:T(8,128)(2,1)}, ...), condition=%wide.region_5.6_spmd, body=%wide.region_2.5_spmd.sunk | while | flops 833714688 | bytes 40163924 | solution.py:92
  159.1 3.4 fusion.132
  167.6 3.4 fusion.132
  176.1 3.4 fusion.132
  184.6 3.4 fusion.132
  188.7 5.0 all-to-all-start.3
  193.9 10.7 %all-to-all-done.3 = bf16[4,512,192]{1,2,0:T(8,128)(2,1)} async-done(((bf16[4,512,192]{1,2,0:T(8,128)(2,1)}), bf16[4,512,192]{1,2,0:T(8,128)(2,1)}, u32[]{:S(2)}, u32[]{:S(2)}) %all-to-all-start.3) | async-done | bytes 786464 | tf_op jit(solution)/shard_map/all_to_all | solution.py:190
  208.5 6.8 fusion.86
  215.3 15.8 %all-gather.11.cloned.1.call-done = bf16[1152,768]{1,0:T(8,128)(2,1)} async-done(((bf16[144,768]{1,0:T(8,128)(2,1)}), bf16[1152,768]{1,0:T(8,128)(2,1)}) %all-gather.11.cloned.1.call-update) | async-done | bytes 1769488 | tf_op jit(solution)/shard_map/all_gather | solution.py:166
  231.1 8.5 %add_convert_fusion = (bf16[512,1152]{1,0:T(8,128)(2,1)S(1)}, f32[512,1152]{1,0:T(8,128)S(1)}, f32[512,1152]{1,0:T(8,128)S(1)}) fusion(f32[512,2304]{1,0:T(8,128)} %fusion.86, bf16[1152,768]{1,0:T(8,128)(2,1)} %all-gather.11.cloned.1.call-done, bf16[1,512,768]{2,1,0:T(8,128)(2,1)S(1)} %copy-done.14), kind=kOutput, calls=%fused_computation.49 | convolution fusion | flops 949026816 | bytes 13172736 | tf_op jit(solution)/shard_map/dot_general | solution.py:25
  246.9 3.9 fusion.74
  250.8 4.3 fusion.70
  255.2 3.0 convolution_convert_fusion
  260.5 5.8 all-to-all-start.4
  266.5 7.1 fusion.64
  273.6 3.5 all-to-all-done.4
  278.1 111.9 %while.28 = (s32[]{:T(128)}, f32[2048,3,64]{0,2,1:T(8,128)S(1)}, f32[2048,3,64]{0,2,1:T(8,128)}, bf16[4,512,192]{1,2,0:T(8,128)(2,1)}, bf16[4,512,3,64]{1,3,2,0:...) while((s32[]{:T(128)}, f32[2048,3,64]{0,2,1:T(8,128)S(1)}, ...), condition=%wide.region_12.13_spmd.clone, body=%wide.region_10.12_spmd.clone.sunk | while | flops 2053175808 | bytes 205107920 | solution.py:139
  280.9 4.5 multiply_reduce_fusion.10
  285.4 4.8 multiply_convert_fusion.7
  290.2 4.4 fusion.143
  294.7 5.6 fusion.145
  300.9 4.6 fusion.144
  308.3 4.5 multiply_reduce_fusion.10
  312.9 4.8 multiply_convert_fusion.7
  317.7 4.4 fusion.143
  322.1 5.6 fusion.145
  328.4 5.2 fusion.144
  336.4 4.5 multiply_reduce_fusion.10
  341.0 4.8 multiply_convert_fusion.7
  345.8 4.5 fusion.143
  350.3 5.7 fusion.145
  356.7 5.2 fusion.144
  364.7 4.5 multiply_reduce_fusion.10
  369.2 4.8 multiply_convert_fusion.7
  374.0 4.4 fusion.143
  378.5 5.6 fusion.145
  384.7 5.2 fusion.144
  390.8 14.3 %all_to_all.116 = bf16[4,512,192]{1,2,0:T(8,128)(2,1)S(1)} all-to-all(bf16[4,512,192]{1,2,0:T(8,128)(2,1)S(1)} %copy.61), channel_id=1, replica_groups=mesh['seq'=4,'fsdp'=8] {'seq'}, dimensions={0} | all-to-all | bytes 1572864 | tf_op jit(solution)/shard_map/all_to_all | solution.py:230
  405.2 4.8 all-to-all-start.5
  413.2 7.5 %all-to-all-done.5 = bf16[4,512,192]{1,2,0:T(8,128)(2,1)S(1)} async-done(((bf16[4,512,192]{1,2,0:T(8,128)(2,1)}), bf16[4,512,192]{1,2,0:T(8,128)(2,1)S(1)}, u32[]{:S(2)}, u32[]{:S(2)}) %all-to-all-start.5) | async-done | bytes 786464 | tf_op jit(solution)/shard_map/all_to_all | solution.py:229
  420.8 4.9 all-to-all-start.7
  429.3 7.3 %all-to-all-done.7 = bf16[4,512,192]{1,2,0:T(8,128)(2,1)} async-done(((bf16[4,512,192]{1,2,0:T(8,128)(2,1)}), bf16[4,512,192]{1,2,0:T(8,128)(2,1)}, u32[]{:S(2)}, u32[]{:S(2)}) %all-to-all-start.7) | async-done | bytes 786464 | tf_op jit(solution)/shard_map/all_to_all | solution.py:231
  436.6 6.6 fusion.67
  445.2 3.7 fusion.66
  448.9 4.7 fusion.58
  457.1 75.9 %reduce-scatter.9.cloned.1.call-done = f32[96,2304]{1,0:T(8,128)} async-done(((f32[768,2304]{1,0:T(8,128)}), f32[96,2304]{1,0:T(8,128)}) %reduce-scatter.9.cloned.1.call-update) | async-done | bytes 884752 | tf_op jit(solution)/shard_map/reduce_scatter | solution.py:249
  535.0 130.2 %reduce-scatter.5.cloned.1.call-done = f32[96,2304]{1,0:T(8,128)} async-done(((f32[768,2304]{1,0:T(8,128)}), f32[96,2304]{1,0:T(8,128)}) %reduce-scatter.5.cloned.1.call-update) | async-done | bytes 884752 | tf_op jit(solution)/shard_map/reduce_scatter | solution.py:246
  667.2 17.1 %all-reduce.4 = (bf16[768]{0:T(1024)(128)(2,1)S(1)}, bf16[768]{0:T(1024)(128)(2,1)S(1)}) all-reduce(f32[768]{0:T(1024)S(1)} %get-tuple-element.127, f32[768]{0:T(1024)S(1)} %copy-done.32), channel_id=2, replica_groups=mesh['seq'=4,'fsdp'=8] {'fsdp'}, use_global_device_ids=true, to_apply=%region_16.17.clone | all-reduce | flops 1536 | bytes 9216
  684.5 9.2 %all-reduce.6 = (bf16[96]{0:T(256)(128)(2,1)S(1)}, bf16[96]{0:T(256)(128)(2,1)S(1)}) all-reduce(bf16[96]{0:T(256)(128)(2,1)S(1)} %dynamic-slice.9, bf16[96]{0:T(256)(128)(2,1)S(1)} %dynamic-slice.8), channel_id=1, replica_groups=mesh['seq'=4,'fsdp'=8] {'seq'}, use_global_device_ids=true, to_apply=%region_17.18 | all-reduce | flops 192 | bytes 768 | tf_op jit(solution)/shard_map/psum | solution.py:253
  697.6 9.9 %all-reduce.10.cloned.1.call-done = (bf16[96,2304]{1,0:T(8,128)(2,1)}, bf16[96,768]{1,0:T(8,128)(2,1)}, bf16[96,2304]{1,0:T(8,128)(2,1)}, bf16[144,768]{1,0:T(8,128)(2,1)}) async-done(((bf16[96,2304]{1,0:T(8,128)(2,1)}, bf16[96,768]{1,0:T(8,128)(2,1)}, bf16[96,2304]{1,0:T(8,128)(2,1)}, bf16[144,768]{1,0:T(8,128)(2,1)}), (bf16[96,2304]{1,0:T(8,128)(2,1)}, bf16[96,768]{1,0:T(8,128)(2,1)}, ...) | async-done | bytes 1253392 | tf_op jit(solution)/shard_map/psum | solution.py:254
  (204 shorter events, 106.9 us)
Async XLA Ops:
  7.2 69.6 %all-gather.5.cloned.1.call-start = ((), (), s32[]{:S(2)}) async-start(), calls=%async_computation.12 | async-start | bytes 3981312 | tf_op jit(solution)/shard_map/all_gather | solution.py:162
  7.9 186.0 %all-gather.7.cloned.1.call-start = ((), (), s32[]{:S(2)}) async-start(), calls=%async_computation.13 | async-start | bytes 1327104 | tf_op jit(solution)/shard_map/all_gather | solution.py:163
  8.6 199.9 %all-gather.9.cloned.1.call-start = ((), (), s32[]{:S(2)}) async-start(), calls=%async_computation.14 | async-start | bytes 3981312 | tf_op jit(solution)/shard_map/all_gather | solution.py:165
  32.2 44.6 %copy-start.28 = (f32[768]{0:T(1024)}, f32[768]{0:T(1024)S(1)}, u32[]{:S(2)}) copy-start(f32[768]{0:T(1024)S(1)} %convert_element_type.162) | copy-start | bytes 9220
  32.5 1.4 copy-start.19
  32.5 60.0 %copy-start.17 = (f32[512,64]{0,1:T(8,128)}, f32[512,64]{0,1:T(8,128)S(1)}, u32[]{:S(2)}) copy-start(f32[512,64]{0,1:T(8,128)S(1)} %get-tuple-element.198) | copy-start | bytes 393220
  32.5 3.3 copy-start.9
  36.0 44.8 %copy-start.26 = (f32[512]{0:T(512)}, f32[512]{0:T(512)S(1)}, u32[]{:S(2)}) copy-start(f32[512]{0:T(512)S(1)} %broadcast_multiply_fusion.8) | copy-start | bytes 6148
  36.4 44.5 %copy-start.30 = (f32[512]{0:T(512)}, f32[512]{0:T(512)S(1)}, u32[]{:S(2)}) copy-start(f32[512]{0:T(512)S(1)} %add_rsqrt_fusion.1) | copy-start | bytes 6148
  80.9 3.2 copy-start.8
  107.4 16.1 %all-to-all-start.1 = ((bf16[512,4,192]{0,2,1:T(8,128)(2,1)}), bf16[512,4,192]{0,2,1:T(8,128)(2,1)S(1)}, u32[]{:S(2)}, u32[]{:S(2)}) async-start(bf16[512,4,192]{0,2,1:T(8,128)(2,1)} %bitcast.14), calls=%async_computation.1 | async-start | bytes 1572864 | tf_op jit(solution)/shard_map/all_to_all | solution.py:186
  123.5 15.2 %all-to-all-start.2 = ((bf16[512,4,192]{0,2,1:T(8,128)(2,1)}), bf16[512,4,192]{0,2,1:T(8,128)(2,1)S(1)}, u32[]{:S(2)}, u32[]{:S(2)}) async-start(bf16[512,4,192]{0,2,1:T(8,128)(2,1)} %bitcast.216), calls=%async_computation.2 | async-start | bytes 1572864 | tf_op jit(solution)/shard_map/all_to_all | solution.py:187
  138.7 15.0 %all-to-all-start = ((bf16[512,4,192]{0,2,1:T(8,128)(2,1)}), bf16[512,4,192]{0,2,1:T(8,128)(2,1)S(1)}, u32[]{:S(2)}, u32[]{:S(2)}) async-start(bf16[512,4,192]{0,2,1:T(8,128)(2,1)} %bitcast.215), calls=%async_computation | async-start | bytes 1572864 | tf_op jit(solution)/shard_map/all_to_all | solution.py:185
  143.0 88.2 %all-gather.11.cloned.1.call-start = ((), (), s32[]{:S(2)}) async-start(), calls=%async_computation.15 | async-start | bytes 1990656 | tf_op jit(solution)/shard_map/all_gather | solution.py:166
  188.7 18.3 %copy-start.2 = (bf16[4,512,3,64]{1,3,2,0:T(8,128)(2,1)}, bf16[4,512,3,64]{1,3,2,0:T(8,128)(2,1)S(1)}, u32[]{:S(2)}) copy-start(bf16[4,512,3,64]{1,3,2,0:T(8,128)(2,1)S(1)} %get-tuple-element.385) | copy-start | bytes 2359300
  188.7 15.9 %all-to-all-start.3 = ((bf16[4,512,192]{1,2,0:T(8,128)(2,1)}), bf16[4,512,192]{1,2,0:T(8,128)(2,1)}, u32[]{:S(2)}, u32[]{:S(2)}) async-start(bf16[4,512,192]{1,2,0:T(8,128)(2,1)} %get-tuple-element.90), calls=%async_computation.3 | async-start | bytes 1572864 | tf_op jit(solution)/shard_map/all_to_all | solution.py:190
  193.7 259.9 %reduce-scatter.7.cloned.1.call-start = ((), (), s32[]{:S(2)}) async-start(), calls=%async_computation.17 | async-start | bytes 2654208 | tf_op jit(solution)/shard_map/reduce_scatter | solution.py:247
  207.0 1.2 copy-start.3
  208.5 22.7 %copy-start.14 = (bf16[1,512,768]{2,1,0:T(8,128)(2,1)S(1)}, bf16[1,512,768]{2,1,0:T(8,128)(2,1)}, u32[]{:S(2)}) copy-start(bf16[1,512,768]{2,1,0:T(8,128)(2,1)} %param.19) | copy-start | bytes 2359300
  231.1 8.5 %copy-start.13 = (f32[512,2304]{1,0:T(8,128)S(1)}, f32[512,2304]{1,0:T(8,128)}, u32[]{:S(2)}) copy-start(f32[512,2304]{1,0:T(8,128)} %fusion.86) | copy-start | bytes 14155780
  239.6 1.6 copy-start.16
  239.7 2.3 copy-start.4
  239.7 3.7 copy-start.34
  241.3 5.0 copy-start.12
  243.4 2.8 copy-start.15
  246.9 8.3 %copy-start.6 = (f32[512,768]{1,0:T(8,128)}, f32[512,768]{1,0:T(8,128)S(1)}, u32[]{:S(2)}) copy-start(f32[512,768]{1,0:T(8,128)S(1)} %multiply_add_fusion) | copy-start | bytes 4718596
  250.8 204.5 %reduce-scatter.11.cloned.1.call-start = ((), (), s32[]{:S(2)}) async-start(), calls=%async_computation.19 | async-start | bytes 3981312 | tf_op jit(solution)/shard_map/reduce_scatter | solution.py:250
  260.5 16.7 %all-to-all-start.4 = ((bf16[512,4,192]{0,2,1:T(8,128)(2,1)}), bf16[512,4,192]{0,2,1:T(8,128)(2,1)}, u32[]{:S(2)}, u32[]{:S(2)}) async-start(bf16[512,4,192]{0,2,1:T(8,128)(2,1)} %bitcast.23), calls=%async_computation.4 | async-start | bytes 1572864 | tf_op jit(solution)/shard_map/all_to_all | solution.py:224
  266.3 266.7 %reduce-scatter.9.cloned.1.call-start = ((), (), s32[]{:S(2)}) async-start(), calls=%async_computation.18 | async-start | bytes 7962624 | tf_op jit(solution)/shard_map/reduce_scatter | solution.py:249
  280.8 4.6 copy-start
  290.2 10.7 %copy-start.1 = (f32[3,512,2048]{2,1,0:T(8,128)S(1)}, f32[3,512,2048]{2,1,0:T(8,128)}, u32[]{:S(2)}) copy-start(f32[3,512,2048]{2,1,0:T(8,128)} %copy-done) | copy-start | bytes 37748740 | tf_op jit(solution)/shard_map/while
  308.3 4.6 copy-start
  317.7 10.7 %copy-start.1 = (f32[3,512,2048]{2,1,0:T(8,128)S(1)}, f32[3,512,2048]{2,1,0:T(8,128)}, u32[]{:S(2)}) copy-start(f32[3,512,2048]{2,1,0:T(8,128)} %copy-done) | copy-start | bytes 37748740 | tf_op jit(solution)/shard_map/while
  336.4 4.6 copy-start
  345.8 10.9 %copy-start.1 = (f32[3,512,2048]{2,1,0:T(8,128)S(1)}, f32[3,512,2048]{2,1,0:T(8,128)}, u32[]{:S(2)}) copy-start(f32[3,512,2048]{2,1,0:T(8,128)} %copy-done) | copy-start | bytes 37748740 | tf_op jit(solution)/shard_map/while
  364.6 4.6 copy-start
  374.0 10.7 %copy-start.1 = (f32[3,512,2048]{2,1,0:T(8,128)S(1)}, f32[3,512,2048]{2,1,0:T(8,128)}, u32[]{:S(2)}) copy-start(f32[3,512,2048]{2,1,0:T(8,128)} %copy-done) | copy-start | bytes 37748740 | tf_op jit(solution)/shard_map/while
  405.2 15.6 %all-to-all-start.5 = ((bf16[4,512,192]{1,2,0:T(8,128)(2,1)}), bf16[4,512,192]{1,2,0:T(8,128)(2,1)S(1)}, u32[]{:S(2)}, u32[]{:S(2)}) async-start(bf16[4,512,192]{1,2,0:T(8,128)(2,1)} %get-tuple-element.92), calls=%async_computation.5 | async-start | bytes 1572864 | tf_op jit(solution)/shard_map/all_to_all | solution.py:229
  413.2 12.7 %copy-start.18 = (f32[512,64]{0,1:T(8,128)S(1)}, f32[512,64]{0,1:T(8,128)}, u32[]{:S(2)}) copy-start(f32[512,64]{0,1:T(8,128)} %copy-done.17) | copy-start | bytes 393220
  420.8 15.8 %all-to-all-start.7 = ((bf16[4,512,192]{1,2,0:T(8,128)(2,1)}), bf16[4,512,192]{1,2,0:T(8,128)(2,1)}, u32[]{:S(2)}, u32[]{:S(2)}) async-start(bf16[4,512,192]{1,2,0:T(8,128)(2,1)} %copy.62), calls=%async_computation.7 | async-start | bytes 1572864 | tf_op jit(solution)/shard_map/all_to_all | solution.py:231
  425.7 239.5 %reduce-scatter.5.cloned.1.call-start = ((), (), s32[]{:S(2)}) async-start(), calls=%async_computation.16 | async-start | bytes 7962624 | tf_op jit(solution)/shard_map/reduce_scatter | solution.py:246
  426.8 0.9 copy-start.20
  427.7 8.9 %copy-start.10 = (bf16[1,512,768]{2,1,0:T(8,128)(2,1)S(1)}, bf16[1,512,768]{2,1,0:T(8,128)(2,1)}, u32[]{:S(2)}) copy-start(bf16[1,512,768]{2,1,0:T(8,128)(2,1)} %param.12) | copy-start | bytes 2359300
  427.7 8.9 %copy-start.27 = (f32[512]{0:T(512)S(1)}, f32[512]{0:T(512)}, u32[]{:S(2)}) copy-start(f32[512]{0:T(512)} %copy-done.26) | copy-start | bytes 6148
  427.7 8.9 %copy-start.29 = (f32[768]{0:T(1024)S(1)}, f32[768]{0:T(1024)}, u32[]{:S(2)}) copy-start(f32[768]{0:T(1024)} %copy-done.28) | copy-start | bytes 9220
  427.7 8.9 %copy-start.31 = (f32[512]{0:T(512)S(1)}, f32[512]{0:T(512)}, u32[]{:S(2)}) copy-start(f32[512]{0:T(512)} %copy-done.30) | copy-start | bytes 6148
  429.3 13.9 %copy-start.21 = (bf16[512,768]{0,1:T(8,128)(2,1)}, bf16[512,768]{0,1:T(8,128)(2,1)S(1)}, u32[]{:S(2)}) copy-start(bf16[512,768]{0,1:T(8,128)(2,1)S(1)} %get-tuple-element.191) | copy-start | bytes 2359300
  443.2 1.6 copy-start.5
  443.2 2.0 copy-start.11
  443.2 264.2 %all-reduce.10.cloned.1.call-start = ((), (), s32[]{:S(2)}) async-start(), calls=%async_computation.20 | async-start | bytes 2506752 | tf_op jit(solution)/shard_map/psum | solution.py:254
  445.2 3.7 copy-start.22
  445.2 3.7 copy-start.23
  445.2 3.7 copy-start.33
  455.3 211.9 %copy-start.32 = (f32[768]{0:T(1024)S(1)}, f32[768]{0:T(1024)}, u32[]{:S(2)}) copy-start(f32[768]{0:T(1024)} %get-tuple-element.125) | copy-start | bytes 9220
  455.3 239.4 %copy-start.7 = (f32[512,768]{1,0:T(8,128)S(1)}, f32[512,768]{1,0:T(8,128)}, u32[]{:S(2)}) copy-start(f32[512,768]{1,0:T(8,128)} %copy-done.6) | copy-start | bytes 4718596
  707.5 4.0 copy-start.24
  707.5 4.8 copy-start.25
Sparse Core Ops, SparseCore 0:
  10.2 66.4 all-gather.4
  78.9 39.2 all-gather.6
  120.4 64.2 all-gather.8
  186.7 44.3 all-gather.10
  250.9 67.9 reduce-scatter.6
  322.4 78.9 reduce-scatter.10
  405.0 127.9 reduce-scatter.8
  537.1 128.0 reduce-scatter.4
  668.4 39.0 all-reduce.9
where the time goes:
time: 729 us; the launch traced here: 720 us
  waiting for transfers between devices  324 us (44%)
  matrix products  169 us (23%)
  other arithmetic  62.8 us (9%)
  blocking collectives  59.7 us (8%)
  local copies, waits for them, and re-layouts  52.5 us (7%)
  starting transfers between devices  35.3 us (5%)
  between operations  16.2 us (2%)
    reduce_scatter x1, waiting for transfers between devices, body(): lax.psum_scatter(grad_w_qkv, 'fsdp', scatter_dimension=0, tiled=True)  130 us
    reduce_scatter x1, waiting for transfers between devices, body(): lax.psum_scatter(grad_w_in, 'fsdp', scatter_dimension=0, tiled=True)  75.9 us
    all_gather x1, waiting for transfers between devices, body(): lax.all_gather(qkv_weight, 'fsdp', axis=0, tiled=True)  40.3 us
    unnamed x2, blocking collectives  36.2 us
    dot_general x4, matrix products, one_block(): jnp.einsum('hqk,khd->qhd', score_grad, key_heads, preferred_element_type=...  22.3 us
    dot_general x4, matrix products, left_contract(): lax.dot_general(left, right, (((0,), (0,)), ((), ())), preferred_element_...  21.9 us
    dot_general x4, matrix products, one_block(): jnp.einsum('hqk,qhd->khd', probs_low, grad_block, preferred_element_type=...  20.3 us
    convert_element_type x4, other arithmetic, one_block(): score_grad = (probs * (prob_grad - centre)).astype(jnp.bfloat16)  19.2 us
  transfers between devices with their start and end apart: 16, of which 12 were waited for; matrix products, arithmetic and copies ran while one was open for 35% of the time, Pallas kernels for 0%

commit v1 on v0

v1 whole, which is shorter than its diff:
```python
import functools
import jax, jax.numpy as jnp
from jax import lax
from jax.experimental import pallas as pl
from jax.experimental.pallas import tpu as pltpu

from jax.sharding import PartitionSpec as P

HEADS = 12
HEAD = 64
PAD = 128
VMEM = 56 * 1024 * 1024

def _dot(a, b, ca, cb):
    return lax.dot_general(a, b, (((ca,), (cb,)), ((), ())), preferred_element_type=jnp.float32)

def _half_turn(v):
    lane = lax.broadcasted_iota(jnp.int32, v.shape, 1)
    ahead = pltpu.roll(v, v.shape[1] - HEAD // 2, 1)
    behind = pltpu.roll(v, HEAD // 2, 1)
    return jnp.where(lane % HEAD < HEAD // 2, ahead, behind)

def project_kernel(heads, x_ref, gain_ref, w_ref, cos_ref, sin_ref, normed_ref, q_ref, k_ref, v_ref):
    x = x_ref[...].astype(jnp.float32)
    centred = x - jnp.mean(x, axis=1, keepdims=True)
    variance = jnp.mean(centred * centred, axis=1, keepdims=True)
    normed = (centred * lax.rsqrt(variance + 1e-5) * gain_ref[...]).astype(jnp.bfloat16)
    normed_ref[...] = normed
    qkv = _dot(normed, w_ref[...], 1, 0)
    span = heads * HEAD
    qk = qkv[:, : 2 * span]
    cos = jnp.concatenate([cos_ref[...]] * heads, axis=1)
    sin = jnp.concatenate([sin_ref[...]] * heads, axis=1)
    qk = qk * cos + _half_turn(qk) * sin
    rows = x.shape[0]
    zeros = jnp.zeros((rows, PAD - HEAD), jnp.bfloat16)
    ones = jnp.where(lax.broadcasted_iota(jnp.int32, (rows, PAD - HEAD), 1) < 3, 1.0, 0.0).astype(jnp.bfloat16)
    for h in range(heads):
        at = slice(h * PAD, (h + 1) * PAD)
        lo = h * HEAD
        q_ref[:, at] = jnp.concatenate([(qk[:, lo : lo + HEAD] * HEAD ** -0.5).astype(jnp.bfloat16), zeros], axis=1)
        k_ref[:, at] = jnp.concatenate([qk[:, span + lo : span + lo + HEAD].astype(jnp.bfloat16), ones], axis=1)
        v_ref[:, at] = jnp.concatenate([qkv[:, 2 * span + lo : 2 * span + lo + HEAD].astype(jnp.bfloat16), ones], axis=1)

def project(x, gain, w, cos, sin, heads, block=512):
    length, width = x.shape
    row = lambda n: pl.BlockSpec((block, n), lambda i: (i, 0))
    whole = lambda a: pl.BlockSpec(a.shape, lambda i: (0, 0))
    outs = [jax.ShapeDtypeStruct((length, width), jnp.bfloat16)] + [jax.ShapeDtypeStruct((length, heads * PAD), jnp.bfloat16)] * 3
    return pl.pallas_call(
        functools.partial(project_kernel, heads),
        grid=(length // block,),
        in_specs=[row(width), whole(gain), whole(w), row(cos.shape[1]), row(sin.shape[1])],
        out_specs=[row(width)] + [row(heads * PAD)] * 3,
        out_shape=outs,
        compiler_params=pltpu.CompilerParams(vmem_limit_bytes=VMEM),
        name="project",
    )(x, gain, w, cos, sin)

def _parts(v):
    high = v.astype(jnp.bfloat16)
    rest = v - high.astype(jnp.float32)
    mid = rest.astype(jnp.bfloat16)
    low = (rest - mid.astype(jnp.float32)).astype(jnp.bfloat16)
    return high, mid, low

def _with_parts(base, v):
    rows = base.shape[0]
    high, mid, low = _parts(v)
    lane = lax.broadcasted_iota(jnp.int32, (rows, PAD - HEAD), 1)
    f = lambda p: p.astype(jnp.float32)
    tail = jnp.where(lane == 0, f(high), jnp.where(lane == 1, f(mid), jnp.where(lane == 2, f(low), 0.0)))
    return jnp.concatenate([base[:, :HEAD], tail.astype(jnp.bfloat16)], axis=1)

def forward_kernel(heads, q_ref, k_ref, v_ref, ctx_ref, out_ref, qx_ref):
    outs = []
    for h in range(heads):
        at = slice(h * PAD, (h + 1) * PAD)
        q = q_ref[:, at]
        scores = _dot(q, k_ref[:, at], 1, 1)
        top = jnp.max(scores, axis=1, keepdims=True)
        weights = jnp.exp(scores - top).astype(jnp.bfloat16)
        sums = _dot(weights, v_ref[:, at], 1, 0)
        total = sums[:, HEAD : HEAD + 1]
        outs.append(sums[:, :HEAD] / total)
        qx_ref[:, at] = _with_parts(q, -(top + jnp.log(total)))
    out = jnp.concatenate(outs, axis=1)
    out_ref[...] = out
    ctx_ref[...] = out.astype(jnp.bfloat16)

def attend_forward(q, k, v, heads, block=512):
    length = q.shape[0]
    row = lambda n: pl.BlockSpec((block, n), lambda i: (i, 0))
    whole = lambda a: pl.BlockSpec(a.shape, lambda i: (0, 0))
    return pl.pallas_call(
        functools.partial(forward_kernel, heads),
        grid=(length // block,),
        in_specs=[row(heads * PAD), whole(k), whole(v)],
        out_specs=[row(heads * HEAD), row(heads * HEAD), row(heads * PAD)],
        out_shape=[jax.ShapeDtypeStruct((length, heads * HEAD), jnp.bfloat16), jax.ShapeDtypeStruct((length, heads * HEAD), jnp.float32), jax.ShapeDtypeStruct((length, heads * PAD), jnp.bfloat16)],
        compiler_params=pltpu.CompilerParams(vmem_limit_bytes=VMEM),
        name="attend_forward",
    )(q, k, v)

def backward_kernel(heads, q_ref, k_ref, v_ref, do_ref, out_ref, dq_ref, dk_ref, dv_ref, dk_acc, dv_acc):
    step = pl.program_id(0)

    @pl.when(step == 0)
    def _():
        dk_acc[...] = jnp.zeros_like(dk_acc)
        dv_acc[...] = jnp.zeros_like(dv_acc)

    do_all = do_ref[...]
    prod = do_all.astype(jnp.float32) * out_ref[...]
    dqs = []
    for h in range(heads):
        at = slice(h * PAD, (h + 1) * PAD)
        lo = h * HEAD
        q, k, v = q_ref[:, at], k_ref[:, at], v_ref[:, at]
        delta = jnp.sum(prod[:, lo : lo + HEAD], axis=1, keepdims=True)
        do = _with_parts(do_all[:, lo : lo + HEAD], -delta)
        probs = jnp.exp(_dot(k, q, 1, 1))
        back = _dot(v, do, 1, 1)
        score_back = (probs * back).astype(jnp.bfloat16)
        dv_acc[:, at] += _dot(probs.astype(jnp.bfloat16), do, 1, 0)
        dk_acc[:, at] += _dot(score_back, q, 1, 0)
        dqs.append(_dot(score_back, k, 0, 0)[:, :HEAD])
    dq_ref[...] = (jnp.concatenate(dqs, axis=1) * HEAD ** -0.5).astype(jnp.bfloat16)

    @pl.when(step == pl.num_programs(0) - 1)
    def _():
        pick = lambda acc: jnp.concatenate([acc[:, h * PAD : h * PAD + HEAD] for h in range(heads)], axis=1).astype(jnp.bfloat16)
        dk_ref[...] = pick(dk_acc)
        dv_ref[...] = pick(dv_acc)

def attend_backward(q, k, v, do, out, heads, block=512):
    length = q.shape[0]
    row = lambda n: pl.BlockSpec((block, n), lambda i: (i, 0))
    whole = lambda n: pl.BlockSpec((length, n), lambda i: (0, 0))
    span = heads * HEAD
    return pl.pallas_call(
        functools.partial(backward_kernel, heads),
        grid=(length // block,),
        in_specs=[row(heads * PAD), whole(heads * PAD), whole(heads * PAD), row(span), row(span)],
        out_specs=[row(span), whole(span), whole(span)],
        out_shape=[jax.ShapeDtypeStruct((length, span), jnp.bfloat16)] * 3,
        scratch_shapes=[pltpu.VMEM((length, heads * PAD), jnp.float32)] * 2,
        compiler_params=pltpu.CompilerParams(vmem_limit_bytes=VMEM),
        name="attend_backward",
    )(q, k, v, do, out)

def weights_kernel(heads, dq_ref, dk_ref, dv_ref, cos_ref, sin_ref, normed_ref, w_ref, back_ref, grad_ref, acc):
    step = pl.program_id(0)

    @pl.when(step == 0)
    def _():
        acc[...] = jnp.zeros_like(acc)

    cos = jnp.concatenate([cos_ref[...]] * heads, axis=1)
    sin = jnp.concatenate([sin_ref[...]] * heads, axis=1)
    qk = jnp.concatenate([dq_ref[...], dk_ref[...]], axis=1).astype(jnp.float32)
    qk = (qk * cos - _half_turn(qk) * sin).astype(jnp.bfloat16)
    grads = jnp.concatenate([qk, dv_ref[...]], axis=1)
    back_ref[...] = _dot(grads, w_ref[...], 1, 1).astype(jnp.bfloat16)
    acc[...] += _dot(normed_ref[...], grads, 0, 0)

    @pl.when(step == pl.num_programs(0) - 1)
    def _():
        grad_ref[...] = acc[...].astype(jnp.bfloat16)

def project_back(dq, dk, dv, cos, sin, normed, w, heads, block=512):
    length, width = normed.shape
    row = lambda n: pl.BlockSpec((block, n), lambda i: (i, 0))
    whole = lambda a: pl.BlockSpec(a.shape, lambda i: (0, 0))
    span = heads * HEAD
    return pl.pallas_call(
        functools.partial(weights_kernel, heads),
        grid=(length // block,),
        in_specs=[row(span)] * 3 + [row(cos.shape[1]), row(sin.shape[1]), row(width), whole(w)],
        out_specs=[row(width), whole(w)],
        out_shape=[jax.ShapeDtypeStruct((length, width), jnp.bfloat16), jax.ShapeDtypeStruct(w.shape, jnp.bfloat16)],
        scratch_shapes=[pltpu.VMEM(w.shape, jnp.float32)],
        compiler_params=pltpu.CompilerParams(vmem_limit_bytes=VMEM),
        name="project_back",
    )(dq, dk, dv, cos, sin, normed, w)


def exchange(value, axis, distance):
    size = lax.axis_size(axis)
    return lax.ppermute(value, axis, [(i, i ^ distance) for i in range(size)])


def gather_rows(piece, axis):
    size = lax.axis_size(axis)
    here = lax.axis_index(axis)
    pieces, order = piece[None], [0]
    distance = size // 2
    while distance:
        pieces = jnp.concatenate([pieces, exchange(pieces, axis, distance)], axis=0)
        order = order + [place ^ distance for place in order]
        distance //= 2
    where = jnp.asarray([order.index(place) for place in range(size)], jnp.int32)
    spots = where[here ^ jnp.arange(size)]
    return jnp.stack([lax.dynamic_index_in_dim(pieces, spots[place], 0, keepdims=False) for place in range(size)])


def halve(value, axis, bit, dim):
    own = (lax.axis_index(axis) >> bit) & 1
    kept = lax.dynamic_index_in_dim(value, own, dim, keepdims=False)
    sent = lax.dynamic_index_in_dim(value, 1 - own, dim, keepdims=False)
    arrived = exchange(sent, axis, 1 << bit)
    return (kept.astype(jnp.float32) + arrived.astype(jnp.float32)).astype(jnp.bfloat16)


def scatter_rows(value, axis):
    bits = lax.axis_size(axis).bit_length() - 1
    rest = value.shape[1:]
    value = value.reshape((2,) * bits + rest)
    for bit in range(bits):
        value = halve(value, axis, bit, bits - 1 - bit)
    return value


EPSILON = 1e-05
ROPE_BASE = 160000.0


def matmul(left, right):
    return jnp.dot(left, right, preferred_element_type=jnp.float32)


def left_contract(left, right):
    return _dot(left, right, 0, 0)


def right_contract(left, right):
    return _dot(left, right, 1, 1)


def normalize(values):
    centred = values - jnp.mean(values, axis=1, keepdims=True)
    variance = jnp.mean(centred * centred, axis=1, keepdims=True)
    scale_inv = lax.rsqrt(variance + EPSILON)
    return (centred * scale_inv, scale_inv)


def norm_back(grad_hat, normed, scale_inv):
    return scale_inv * (
        grad_hat
        - jnp.mean(grad_hat, axis=1, keepdims=True)
        - normed * jnp.mean(grad_hat * normed, axis=1, keepdims=True)
    )


def rope_tables(places):
    half = HEAD // 2
    inverse = ROPE_BASE ** (-(jnp.arange(half, dtype=jnp.float32) * 2.0 / HEAD))
    angles = places[:, None] * inverse[None, :]
    cosine, sine = lax.optimization_barrier((jnp.cos(angles), jnp.sin(angles)))
    return (
        jnp.concatenate([cosine] * 4, axis=1),
        jnp.concatenate([-sine, sine] * 2, axis=1),
    )


def from_slices(block):
    far = exchange(block, "seq", 2)
    return [block, exchange(block, "seq", 1), far, exchange(far, "seq", 1)]


def in_order(blocks, here):
    stacked = jnp.stack(blocks)
    return [lax.dynamic_index_in_dim(stacked, here ^ i, 0, keepdims=False) for i in range(len(blocks))]


def body(
    inputs,
    norm_one,
    qkv_weight,
    attn_out_weight,
    norm_two,
    mlp_in_weight,
    mlp_out_weight,
    cotangent,
):
    here = lax.axis_index("seq")
    slices = lax.axis_size("seq")
    owners = lax.axis_size("fsdp")
    heads = HEADS // slices
    span = heads * HEAD
    rows, width = inputs.shape[1:]
    share = qkv_weight.shape[0]
    hidden_share = mlp_out_weight.shape[0]
    hidden_size = hidden_share * owners

    x = inputs[0]
    own_columns = lax.dynamic_index_in_dim(
        qkv_weight.reshape(share, 3, slices, span), here, 2, keepdims=False
    ).reshape(share, 3 * span)
    gains = jnp.concatenate([norm_one, norm_two, jnp.zeros((3 * span - 2 * share,), jnp.bfloat16)])
    packed = gather_rows(jnp.concatenate([own_columns, gains[None]], axis=0), "fsdp")
    w_qkv = packed[:, :share].reshape(width, 3 * span)
    gain_one = packed[:, share, :share].reshape(1, width).astype(jnp.float32)
    gain_two = packed[:, share, share : 2 * share].reshape(1, width).astype(jnp.float32)
    x_all = jnp.concatenate(from_slices(x), axis=0)

    def whole(weight):
        part = weight.shape[0] // slices
        if part * slices != weight.shape[0]:
            return lax.all_gather(weight, "fsdp", axis=0, tiled=True)
        mine = lax.dynamic_slice_in_dim(weight, here * part, part, 0)
        return lax.all_gather(mine, ("fsdp", "seq"), axis=0, tiled=True)

    w_attn = whole(attn_out_weight)
    w_in = whole(mlp_in_weight)
    w_out = whole(mlp_out_weight)

    order = here ^ jnp.arange(slices)
    places = (order[:, None] * rows + jnp.arange(rows)[None, :]).reshape(-1).astype(jnp.float32)
    cosine, sine = rope_tables(places)

    normed_all, query, key, value = project(x_all, gain_one, w_qkv, cosine, sine, heads)
    context_all, out_all, query = attend_forward(query, key, value, heads)
    context_blocks = context_all.reshape(slices, rows, span)
    context = [context_blocks[0]] + [exchange(context_blocks[j], "seq", j) for j in range(1, slices)]
    context_low = jnp.concatenate(in_order(context, here), axis=1)

    attended = x.astype(jnp.float32) + matmul(context_low, w_attn)
    normed_hat2, scale_two = normalize(attended)
    normed_low2 = (normed_hat2 * gain_two).astype(jnp.bfloat16)
    gate_up = matmul(normed_low2, w_in)
    first_half = gate_up[:, :hidden_size]
    second_half = gate_up[:, hidden_size:]
    gelu_first, gelu_back = jax.vjp(lambda entry: jax.nn.gelu(entry, approximate=False), first_half)
    hidden_low = (gelu_first * second_half).astype(jnp.bfloat16)
    result = (attended + matmul(hidden_low, w_out)).astype(jnp.bfloat16)
    grad_low = cotangent[0]
    grad_w_out = left_contract(hidden_low, grad_low)
    hidden_grad = right_contract(grad_low, w_out)
    first_grad = gelu_back(hidden_grad * second_half)[0]
    second_grad = hidden_grad * gelu_first
    gate_up_grad = jnp.concatenate([first_grad, second_grad], axis=1).astype(jnp.bfloat16)
    grad_w_in = left_contract(normed_low2, gate_up_grad)
    normed_grad2 = right_contract(gate_up_grad, w_in)
    attended_grad = grad_low.astype(jnp.float32) + norm_back(
        normed_grad2 * gain_two, normed_hat2, scale_two
    )
    branch_low = attended_grad.astype(jnp.bfloat16)
    grad_w_attn = left_contract(context_low, branch_low)
    context_grad = right_contract(branch_low, w_attn).astype(jnp.bfloat16)

    grad_blocks = context_grad.reshape(rows, slices, span)
    grad_blocks = [lax.dynamic_index_in_dim(grad_blocks, here ^ j, 1, keepdims=False) for j in range(slices)]
    context_grad_all = jnp.concatenate(
        [grad_blocks[0]] + [exchange(grad_blocks[j], "seq", j) for j in range(1, slices)], axis=0
    )

    mlp_grads = jnp.concatenate(
        [grad_w_attn.reshape(owners, share, width)]
        + [grad_w_in[:, at : at + width].reshape(owners, share, width) for at in range(0, 2 * hidden_size, width)]
        + [grad_w_out.reshape(owners, hidden_share, width)],
        axis=1,
    ).astype(jnp.bfloat16)
    total_rows = mlp_grads.shape[1]
    half = total_rows // 2
    mlp_grads = halve(mlp_grads.reshape(owners, 2, half, width), "seq", 0, 1)
    cut = (half // 2 + 7) // 8 * 8
    one = mlp_grads[:, :cut].reshape(owners, cut, 2, width // 2)
    two = mlp_grads[:, cut:].reshape(owners, half - cut, 2, width // 2)
    one = scatter_rows(halve(one, "seq", 1, 2), "fsdp")
    two = halve(scatter_rows(two, "fsdp"), "seq", 1, 1)
    mlp_part = jnp.concatenate([one, two], axis=0)

    query_grad, key_grad, value_grad = attend_backward(query, key, value, context_grad_all, out_all, heads)
    back_all, grad_w_qkv = project_back(query_grad, key_grad, value_grad, cosine, sine, normed_all, w_qkv, heads)

    back_blocks = back_all.reshape(slices, rows, width)
    back_near = exchange(back_blocks[1::2], "seq", 1)
    back_pair = back_blocks[::2].astype(jnp.float32) + back_near.astype(jnp.float32)
    back_far = exchange(back_pair[1].astype(jnp.bfloat16), "seq", 2)
    normed_grad1 = back_pair[0] + back_far.astype(jnp.float32)

    qkv_part = scatter_rows(grad_w_qkv.reshape(owners, share, 3 * span), "fsdp")

    float_input = x.astype(jnp.float32)
    normed_hat1, scale_one = normalize(float_input)
    input_grad = attended_grad + norm_back(normed_grad1 * gain_one, normed_hat1, scale_one)

    qkv_blocks = in_order(from_slices(qkv_part), here)
    qkv_grad = jnp.stack([b.reshape(share, 3, span) for b in qkv_blocks], axis=2)
    qkv_grad = qkv_grad.reshape(share, 3 * width).astype(jnp.float32)

    mlp_blocks = in_order(from_slices(mlp_part), here)
    mlp_total = jnp.concatenate(
        [jnp.concatenate([mlp_blocks[core], mlp_blocks[2 + core]], axis=1) for core in range(2)], axis=0
    ).astype(jnp.float32)
    attn_grad = mlp_total[:share]
    count = 2 * hidden_size // width
    in_grad = jnp.concatenate([mlp_total[share * (1 + c) : share * (2 + c)] for c in range(count)], axis=1)
    out_grad = mlp_total[share * (1 + count) :]

    gain_grad1 = jnp.sum(qkv_weight.astype(jnp.float32) * qkv_grad, axis=1) / norm_one.astype(jnp.float32)
    gain_grad2 = jnp.sum(mlp_in_weight.astype(jnp.float32) * in_grad, axis=1) / norm_two.astype(jnp.float32)
    return (
        result[None],
        input_grad.astype(jnp.bfloat16)[None],
        gain_grad1,
        qkv_grad,
        attn_grad,
        gain_grad2,
        in_grad,
        out_grad,
    )


def solution(mesh):
    tokens = P("fsdp", "seq", None)
    vector = P("fsdp")
    matrix = P("fsdp", None)
    return jax.shard_map(
        body,
        mesh=mesh,
        in_specs=(tokens, vector, matrix, matrix, vector, matrix, matrix, tokens),
        out_specs=(tokens, tokens, vector, matrix, matrix, vector, matrix, matrix),
        check_vma=False,
    )
```

time: 729 us -> 447 us (0.61)
  waiting for transfers between devices: 324 us -> 129 us
  matrix products: 169 us -> 28.8 us
  Pallas kernels: 0 us -> 82.3 us
  blocking collectives: 59.7 us -> 0 us
  local copies, waits for them, and re-layouts: 52.5 us -> 93.6 us
  other arithmetic: 62.8 us -> 45.9 us
  between operations: 16.2 us -> 30.5 us
    reduce_scatter x4 -> x0, waiting for transfers between devices: 206 us -> none  [the longest x1 130 us: body(): lax.psum_scatter(grad_w_qkv, 'fsdp', scatter_dimension=0, tiled=True)]
    dot_general x36 -> x6, matrix products: 152 us -> 18.5 us  [_dot(): lax.dot_general(a, b, (((ca,), (cb,)), ((), ())), preferred_element_type=...]
    pallas_call x0 -> x4, Pallas kernels: none -> 82.3 us  [the longest x1 38.8 us: attend_backward(): pl.pallas_call(functools.partial(backward_kernel, heads), grid=(length //...]
    ppermute x0 -> x32, waiting for transfers between devices: none -> 72.8 us  [exchange(): return lax.ppermute(value, axis, [(i, i ^ distance) for i in range(size)])]
    all_to_all x7 -> x0, waiting for transfers between devices: 49.9 us -> none  [the longest x1 10.7 us: body(): lax.all_to_all(context_all, 'seq', split_axis=0, concat_axis=1, tiled=True)]
    unnamed x2 -> x0, blocking collectives: 36.2 us -> none
    all_to_all x7 -> x0, starting transfers between devices: 34.3 us -> none  [the longest x1 5.79 us: body(): lax.all_to_all(context_grad, 'seq', split_axis=1, concat_axis=0, tiled=True)]
    ppermute x0 -> x32, starting transfers between devices: none -> 31.1 us  [exchange(): return lax.ppermute(value, axis, [(i, i ^ distance) for i in range(size)])]
  transfers between devices with their start and end apart: 16 -> 35, of which waited for: 12 -> 18; matrix products, arithmetic and copies ran while one was open for 35% -> 29% of each run, Pallas kernels for 0% -> 7%
where the time goes in v1:
time: 447 us; the launch traced here: 441 us
  waiting for transfers between devices  129 us (29%)
  local copies, waits for them, and re-layouts  93.6 us (21%)
  Pallas kernels  82.3 us (18%)
  other arithmetic  45.9 us (10%)
  starting transfers between devices  31.2 us (7%)
  between operations  30.5 us (7%)
  matrix products  28.8 us (6%)
    ppermute x32, waiting for transfers between devices, exchange(): return lax.ppermute(value, axis, [(i, i ^ distance) for i in range(size)])  72.8 us
    all_gather x3, waiting for transfers between devices, whole(): return lax.all_gather(mine, ('fsdp', 'seq'), axis=0, tiled=True)  55.7 us
    pallas_call x1, Pallas kernels, attend_backward(): pl.pallas_call(functools.partial(backward_kernel, heads), grid=(length //...  38.8 us
    ppermute x32, starting transfers between devices, exchange(): return lax.ppermute(value, axis, [(i, i ^ distance) for i in range(size)])  31.1 us
    unnamed x73, local copies, waits for them, and re-layouts  30.3 us
    pallas_call x1, Pallas kernels, attend_forward(): pl.pallas_call(functools.partial(forward_kernel, heads), grid=(length //...  23.8 us
    dot_general x6, matrix products, _dot(): lax.dot_general(a, b, (((ca,), (cb,)), ((), ())), preferred_element_type=...  18.5 us
    pallas_call x1, Pallas kernels, project_back(): pl.pallas_call(functools.partial(weights_kernel, heads), grid=(length //...  10.6 us
  transfers between devices with their start and end apart: 35, of which 18 were waited for; matrix products, arithmetic and copies ran while one was open for 29% of the time, Pallas kernels for 7%

profile of v1, /device:TPU:1, one launch (start us, length us, event | category | flops | bytes accessed | tf_op | source)
XLA Modules:
  0.0 441.0 jit_solution(3804326148958030624)
XLA Ops:
  11.1 2.1 collective-permute-start.1
  17.4 2.4 collective-permute-start.3
  19.8 7.4 %collective-permute-done.3 = bf16[1,97,576]{1,2,0:T(8,128)(2,1)S(1)} collective-permute-done((bf16[1,97,576]{1,2,0:T(8,128)(2,1)S(1)}, bf16[1,97,576]{1,2,0:T(8,128)(2,1)S(1)}, u32[]{:S(2)}, u32[]{:S(2)}) %collective-permute-start.3) | collective-permute-done | bytes 111776 | tf_op jit(solution)/shard_map/ppermute | solution.py:190
  28.0 3.7 multiply_sine_fusion
  31.7 3.6 collective-permute-done.4
  56.6 2.0 collective-permute-start.2
  58.5 4.8 %pad_maximum_fusion.6 = (f32[2048,128]{1,0:T(8,128)}, f32[2048,128]{1,0:T(8,128)}) fusion(f32[2048,32]{1,0:T(8,128)S(1)} %get-tuple-element.22, f32[2048,32]{1,0:T(8,128)S(1)} %get-tuple-element.23, f32[2048,32]{1,0:T(8,128)} %neg.18), kind=kLoop, calls=%fused_computation.67 | loop fusion | flops 1572864 | bytes 2883584 | tf_op jit(solution)/shard_map/concatenate | solution.py:261
  63.8 2.2 pad_maximum_fusion.10
  66.0 2.1 constant_dynamic-slice_fusion.15
  68.1 5.4 %stack.56 = bf16[8,97,576]{2,0,1:T(8,128)(2,1)S(1)} concatenate(bf16[1,97,576]{2,0,1:T(2,128)(2,1)S(1)} %get-tuple-element.72, bf16[1,97,576]{2,0,1:T(2,128)(2,1)S(1)} %get-tuple-element.71, bf16[1,97,576]{2,0,1:T(2,128)(2,1)S(1)} %get-tuple-element.70, bf16[1,97,576]{2,0,1:T(2,128)(2,1)S(1)} %get-tuple-element.69, bf16[1,97,576]{2,0,1:T(2,128)(2,1)S(1)} %get-tuple-element.68, ...), dimensions={0} | concatenate | bytes 1787904 | tf_op jit(solution)/shard_map/stack | solution.py:204
  75.4 3.1 pad_maximum_fusion.x_ref
  78.5 9.0 %project.1 = (bf16[2048,768]{1,0:T(8,128)(2,1)}, bf16[2048,384]{1,0:T(8,128)(2,1)}, bf16[2048,384]{1,0:T(8,128)(2,1)}, bf16[2048,384]{1,0:T(8,128)(2,1)}) custom-call(bf16[2048,768]{1,0:T(8,128)(2,1)} %pad_maximum_fusion.x_ref, f32[1,768]{1,0:T(1,128)} %reshape.219.gain_ref, bf16[768,576]{1,0:T(8,128)(2,1)} %bitcast.183, ...), custom_call_target="tpu_custom_call" | custom-call | tf_op jit(solution)/shard_map/project/pallas_call | solution.py:50
  87.5 23.8 %attend_forward.1 = (bf16[2048,192]{1,0:T(8,128)(2,1)}, f32[2048,192]{1,0:T(8,128)}, bf16[2048,384]{1,0:T(8,128)(2,1)}) custom-call(bf16[2048,384]{1,0:T(8,128)(2,1)} %get-tuple-element.24.q_ref, bf16[2048,384]{1,0:T(8,128)(2,1)} %get-tuple-element.25.k_ref, bf16[2048,384]{1,0:T(8,128)(2,1)} %get-tuple-element.26.v_ref), custom_call_target="tpu_custom_call" | custom-call | tf_op jit(solution)/shard_map/attend_forward/pallas_call | solution.py:95
  115.1 8.0 %collective-permute-done.8 = bf16[512,192]{1,0:T(8,128)(2,1)S(1)} collective-permute-done((bf16[512,192]{1,0:T(8,128)(2,1)S(1)}, bf16[512,192]{1,0:T(8,128)(2,1)S(1)}, u32[]{:S(2)}, u32[]{:S(2)}) %collective-permute-start.8) | collective-permute-done | bytes 196640 | tf_op jit(solution)/shard_map/ppermute | solution.py:190
  123.0 5.4 %collective-permute-done.7 = bf16[512,192]{1,0:T(8,128)(2,1)S(1)} collective-permute-done((bf16[512,192]{1,0:T(8,128)(2,1)S(1)}, bf16[512,192]{1,0:T(8,128)(2,1)S(1)}, u32[]{:S(2)}, u32[]{:S(2)}) %collective-permute-start.7) | collective-permute-done | bytes 196640 | tf_op jit(solution)/shard_map/ppermute | solution.py:190
  128.8 2.5 fusion.54
  131.7 4.1 reshape.244
  135.8 55.6 %all-gather.7.cloned.1.call-done = bf16[768,2304]{1,0:T(8,128)(2,1)} async-done(((bf16[24,2304]{1,0:T(8,128)(2,1)}), bf16[768,2304]{1,0:T(8,128)(2,1)}) %all-gather.7.cloned.1.call-update) | async-done | bytes 3538960 | tf_op jit(solution)/shard_map/all_gather | solution.py:312
  191.5 4.2 fusion.49
  195.7 6.1 %add_convert_fusion = (bf16[512,1152]{1,0:T(8,128)(2,1)S(1)}, f32[512,1152]{1,0:T(8,128)S(1)}, f32[512,1152]{1,0:T(8,128)S(1)}) fusion(f32[512,2304]{1,0:T(8,128)S(1)} %fusion.49, bf16[1152,768]{1,0:T(8,128)(2,1)S(1)} %copy-done.11, bf16[1,512,768]{2,1,0:T(8,128)(2,1)S(1)} %copy-done.14), kind=kOutput, calls=%fused_computation.15 | convolution fusion | flops 949026816 | bytes 13172736 | tf_op jit(solution)/shard_map/dot_general | solution.py:15
  202.5 4.0 convolution_convert_fusion
  206.5 2.2 fusion.50
  209.9 2.1 convolution_convert_fusion.1
  212.1 1.7 convolution_convert_fusion.2
  213.8 2.3 copy.62
  216.1 2.1 constant_dynamic-slice_fusion.12
  218.2 1.8 copy.66
  221.2 1.8 copy.65
  223.3 1.8 copy.64
  225.6 2.4 constant_dynamic-update-slice_fusion.3
  228.0 3.3 fusion.52
  233.5 1.8 copy.63
  236.7 2.4 constant_dynamic-update-slice_fusion
  239.2 2.3 pad_maximum_fusion.9.do_ref
  241.4 38.8 %attend_backward.1 = (bf16[2048,192]{1,0:T(8,128)(2,1)}, bf16[2048,192]{1,0:T(8,128)(2,1)}, bf16[2048,192]{1,0:T(8,128)(2,1)}) custom-call(bf16[2048,384]{1,0:T(8,128)(2,1)} %get-tuple-element.28.q_ref, bf16[2048,384]{1,0:T(8,128)(2,1)} %get-tuple-element.25.k_ref, bf16[2048,384]{1,0:T(8,128)(2,1)} %get-tuple-element.26.v_ref, ...), custom_call_target="tpu_custom_call" | custom-call | tf_op jit(solution)/shard_map/attend_backward/pallas_call | solution.py:141
  280.3 10.6 %project_back.1 = (bf16[2048,768]{1,0:T(8,128)(2,1)}, bf16[768,576]{1,0:T(8,128)(2,1)}) custom-call(bf16[2048,192]{1,0:T(8,128)(2,1)} %get-tuple-element.30.dq_ref, bf16[2048,192]{1,0:T(8,128)(2,1)} %get-tuple-element.31.dk_ref, bf16[2048,192]{1,0:T(8,128)(2,1)} %get-tuple-element.32.dv_ref, f32[2048,128]{1,0:T(8,128)} %get-tuple-element.107.cos_ref, ...), custom_call_target="tpu_custom_call" | custom-call | tf_op jit(solution)/shard_map/project_back/pallas_call | solution.py:176
  290.9 2.2 constant_dynamic-slice_fusion.8
  294.3 2.3 convert_dynamic-update-slice_fusion
  296.6 6.1 %constant_dynamic-slice_fusion.3 = (bf16[8,1,264,768]{3,2,1,0:T(8,128)(2,1)}, bf16[8,264,768]{2,1,0:T(8,128)(2,1)}) fusion(bf16[8,2,264,768]{3,2,1,0:T(8,128)(2,1)} %bitcast.56, s32[]{:T(128)S(6)} %select_n.149, s32[]{:T(128)S(6)} %select_n.150), kind=kLoop, calls=%fused_computation.136 | loop fusion | bytes 12976136 | tf_op jit(solution)/shard_map/jit(dynamic_index_in_dim)/dynamic_slice | solution.py:209
  303.2 2.1 copy.81
  306.3 2.1 copy.68
  310.6 2.7 slice.122
  314.3 3.3 collective-permute-done.15
  319.0 8.1 %collective-permute-done.16 = bf16[96,576]{0,1:T(8,128)(2,1)S(1)} collective-permute-done((bf16[96,576]{0,1:T(8,128)(2,1)S(1)}, bf16[96,576]{0,1:T(8,128)(2,1)S(1)}, u32[]{:S(2)}, u32[]{:S(2)}) %collective-permute-start.16) | collective-permute-done | bytes 110624 | tf_op jit(solution)/shard_map/ppermute | solution.py:190
  330.4 2.1 collective-permute-done.18
  332.5 1.9 collective-permute-start.19
  334.4 3.5 fusion.24
  338.0 6.2 %copy.82 = bf16[8,1,264,768]{2,3,0,1:T(8,128)(2,1)} copy(bf16[8,1,264,768]{3,2,1,0:T(8,128)(2,1)} %get-tuple-element.46) | data formatting | bytes 6488064
  347.3 2.5 convert_add_fusion.1
  349.9 1.7 copy-done.5
  353.8 6.3 %copy.72 = bf16[8,264,768]{1,2,0:T(8,128)(2,1)} copy(bf16[8,264,768]{2,1,0:T(8,128)(2,1)} %collective-permute-done.20) | data formatting | bytes 6488064 | tf_op jit(solution)/shard_map/ppermute | solution.py:190
  360.1 4.9 %fusion = bf16[8,264,768]{1,2,0:T(8,128)(2,1)S(1)} fusion(bf16[8,264,768]{1,2,0:T(8,128)(2,1)} %copy.72, bf16[8,1,264,768]{2,3,0,1:T(8,128)(2,1)} %copy.82), kind=kLoop, calls=%fused_computation.2 | loop fusion | flops 6488064 | bytes 9732096 | tf_op jit(solution)/shard_map/convert_element_type | solution.py:212
  370.1 1.9 slice-done
  372.0 2.1 constant_dynamic-slice_fusion.2
  377.2 2.0 fusion.38
  380.4 4.7 %copy.89 = f32[8,136,1,384]{3,2,1,0:T(1,128)S(1)} copy(f32[8,136,1,384]{1,3,2,0:T(8,128)} %get-tuple-element.52) | data formatting | bytes 3342336
  385.2 2.7 collective-permute-done.25
  389.5 5.9 %collective-permute-done.21 = bf16[8,136,384]{2,1,0:T(8,128)(2,1)} collective-permute-done((bf16[8,136,384]{2,1,0:T(8,128)(2,1)}, bf16[8,136,384]{2,1,0:T(8,128)(2,1)}, u32[]{:S(2)}, u32[]{:S(2)}) %collective-permute-start.21) | collective-permute-done | bytes 835616 | tf_op jit(solution)/shard_map/ppermute | solution.py:190
  400.0 6.6 %collective-permute-done.22 = bf16[2,2,136,384]{3,2,1,0:T(8,128)(2,1)S(1)} collective-permute-done((bf16[2,2,136,384]{3,2,1,0:T(8,128)(2,1)S(1)}, bf16[2,2,136,384]{3,2,1,0:T(8,128)(2,1)S(1)}, u32[]{:S(2)}, u32[]{:S(2)}) %collective-permute-start.22) | collective-permute-done | bytes 417824 | tf_op jit(solution)/shard_map/ppermute | solution.py:190
  406.9 4.3 collective-permute-done.27
  411.6 3.0 collective-permute-done.23
  415.1 6.2 %collective-permute-done.24 = bf16[136,384]{1,0:T(8,128)(2,1)S(1)} collective-permute-done((bf16[136,384]{1,0:T(8,128)(2,1)S(1)}, bf16[136,384]{1,0:T(8,128)(2,1)S(1)}, u32[]{:S(2)}, u32[]{:S(2)}) %collective-permute-start.24) | collective-permute-done | bytes 104480 | tf_op jit(solution)/shard_map/ppermute | solution.py:190
  422.9 3.9 collective-permute-done.30
  426.8 2.1 collective-permute-start.31
  (203 shorter events, 67.9 us)
Async XLA Ops:
  7.2 1.6 copy-start
  7.2 121.6 %all-gather.5.cloned.1.call-start = ((), (), s32[]{:S(2)}) async-start(), calls=%async_computation | async-start | bytes 1216512 | tf_op jit(solution)/shard_map/all_gather | solution.py:312
  8.7 123.0 %all-gather.9.cloned.1.call-start = ((), (), s32[]{:S(2)}) async-start(), calls=%async_computation.2 | async-start | bytes 2027520 | tf_op jit(solution)/shard_map/all_gather | solution.py:312
  9.4 182.0 %all-gather.7.cloned.1.call-start = ((), (), s32[]{:S(2)}) async-start(), calls=%async_computation.1 | async-start | bytes 3649536 | tf_op jit(solution)/shard_map/all_gather | solution.py:312
  11.1 45.5 %collective-permute-start.1 = (bf16[512,768]{1,0:T(8,128)(2,1)}, bf16[512,768]{1,0:T(8,128)(2,1)}, u32[]{:S(2)}, u32[]{:S(2)}) collective-permute-start(bf16[512,768]{1,0:T(8,128)(2,1)} %bitcast.179), channel_id=1, source_target_pairs={{0,16},{8,24},{16,0},{24,8},{1,17},{9,25},{17,1},{25,9},{2,18},{10... | collective-permute-start | bytes 2359304 | tf_op jit(solution)/shard_map/ppermute | solution.py:190
  13.2 62.2 %collective-permute-start = (bf16[512,768]{1,0:T(8,128)(2,1)}, bf16[512,768]{1,0:T(8,128)(2,1)}, u32[]{:S(2)}, u32[]{:S(2)}) collective-permute-start(bf16[512,768]{1,0:T(8,128)(2,1)} %bitcast.180), channel_id=1, source_target_pairs={{0,8},{8,0},{16,24},{24,16},{1,9},{9,1},{17,25},{25,17},{2,10},{10... | collective-permute-start | bytes 2359304 | tf_op jit(solution)/shard_map/ppermute | solution.py:190
  17.4 9.8 %collective-permute-start.3 = (bf16[1,97,576]{1,2,0:T(8,128)(2,1)S(1)}, bf16[1,97,576]{1,2,0:T(8,128)(2,1)S(1)}, u32[]{:S(2)}, u32[]{:S(2)}) collective-permute-start(bf16[1,97,576]{1,2,0:T(8,128)(2,1)S(1)} %maximum_bitcast_fusion), channel_id=1, source_target_pairs={{0,4},{1,5},{2,6},{3,7},{4,0},{5,1},{6,2},{7,3},{8,12},{9,13},{10,... | collective-permute-start | bytes 335240 | tf_op jit(solution)/shard_map/ppermute | solution.py:190
  27.3 8.1 %collective-permute-start.4 = (bf16[2,97,576]{1,2,0:T(8,128)(2,1)S(1)}, bf16[2,97,576]{1,2,0:T(8,128)(2,1)S(1)}, u32[]{:S(2)}, u32[]{:S(2)}) collective-permute-start(bf16[2,97,576]{1,2,0:T(8,128)(2,1)S(1)} %pad_maximum_fusion.16), channel_id=1, source_target_pairs={{0,2},{1,3},{2,0},{3,1},{4,6},{5,7},{6,4},{7,5},{8,10},{9,11},{10,... | collective-permute-start | bytes 670472 | tf_op jit(solution)/shard_map/ppermute | solution.py:190
  28.0 10.5 %copy-start.2 = (s32[8]{0:T(128)S(1)}, s32[8]{0:T(128)}, u32[]{:S(2)}) copy-start(s32[8]{0:T(128)} %constant.255.clone) | copy-start | bytes 100
  37.0 26.8 %collective-permute-start.5 = (bf16[4,97,576]{2,0,1:T(4,128)(2,1)}, bf16[4,97,576]{2,0,1:T(4,128)(2,1)}, u32[]{:S(2)}, u32[]{:S(2)}) collective-permute-start(bf16[4,97,576]{2,0,1:T(4,128)(2,1)} %copy.56), channel_id=1, source_target_pairs={{0,1},{1,0},{2,3},{3,2},{4,5},{5,4},{6,7},{7,6},{8,9},{9,8},{10,11... | collective-permute-start | bytes 1340936 | tf_op jit(solution)/shard_map/ppermute | solution.py:190
  56.6 18.9 %collective-permute-start.2 = (bf16[512,768]{1,0:T(8,128)(2,1)}, bf16[512,768]{1,0:T(8,128)(2,1)}, u32[]{:S(2)}, u32[]{:S(2)}) collective-permute-start(bf16[512,768]{1,0:T(8,128)(2,1)} %collective-permute-done.1), channel_id=1, source_target_pairs={{0,8},{8,0},{16,24},{24,16},{1,9},{9,1},{17,25},{25,17},{2,10},{10... | collective-permute-start | bytes 2359304 | tf_op jit(solution)/shard_map/ppermute | solution.py:190
  73.5 1.9 copy-start.3
  112.8 10.2 %collective-permute-start.8 = (bf16[512,192]{1,0:T(8,128)(2,1)S(1)}, bf16[512,192]{1,0:T(8,128)(2,1)S(1)}, u32[]{:S(2)}, u32[]{:S(2)}) collective-permute-start(bf16[512,192]{1,0:T(8,128)(2,1)S(1)} %get-tuple-element.60), channel_id=1, source_target_pairs={{0,24},{8,16},{16,8},{24,0},{1,25},{9,17},{17,9},{25,1},{2,26},{10... | collective-permute-start | bytes 589832 | tf_op jit(solution)/shard_map/ppermute | solution.py:190
  112.9 15.6 %collective-permute-start.7 = (bf16[512,192]{1,0:T(8,128)(2,1)S(1)}, bf16[512,192]{1,0:T(8,128)(2,1)S(1)}, u32[]{:S(2)}, u32[]{:S(2)}) collective-permute-start(bf16[512,192]{1,0:T(8,128)(2,1)S(1)} %get-tuple-element.61), channel_id=1, source_target_pairs={{0,16},{8,24},{16,0},{24,8},{1,17},{9,25},{17,1},{25,9},{2,18},{10... | collective-permute-start | bytes 589832 | tf_op jit(solution)/shard_map/ppermute | solution.py:190
  114.2 14.2 %collective-permute-start.6 = (bf16[512,192]{1,0:T(8,128)(2,1)S(1)}, bf16[512,192]{1,0:T(8,128)(2,1)S(1)}, u32[]{:S(2)}, u32[]{:S(2)}) collective-permute-start(bf16[512,192]{1,0:T(8,128)(2,1)S(1)} %get-tuple-element.62), channel_id=1, source_target_pairs={{0,8},{8,0},{16,24},{24,16},{1,9},{9,1},{17,25},{25,17},{2,10},{10... | collective-permute-start | bytes 589832 | tf_op jit(solution)/shard_map/ppermute | solution.py:190
  128.7 2.6 copy-start.18
  128.8 2.6 copy-start.20
  128.8 2.6 copy-start.22
  128.8 2.6 copy-start.24
  135.8 59.9 %copy-start.14 = (bf16[1,512,768]{2,1,0:T(8,128)(2,1)S(1)}, bf16[1,512,768]{2,1,0:T(8,128)(2,1)}, u32[]{:S(2)}) copy-start(bf16[1,512,768]{2,1,0:T(8,128)(2,1)} %param.16) | copy-start | bytes 2359300
  191.5 4.2 copy-start.11
  202.4 4.0 copy-start.28
  206.5 2.2 copy-start.15
  208.7 1.1 copy-start.23
  208.7 1.2 copy-start.25
  209.9 2.1 copy-start.7
  209.9 2.1 copy-start.29
  219.9 19.3 %collective-permute-start.11 = (bf16[512,192]{1,0:T(8,128)(2,1)}, bf16[512,192]{1,0:T(8,128)(2,1)}, u32[]{:S(2)}, u32[]{:S(2)}) collective-permute-start(bf16[512,192]{1,0:T(8,128)(2,1)} %bitcast.206), channel_id=1, source_target_pairs={{0,24},{8,16},{16,8},{24,0},{1,25},{9,17},{17,9},{25,1},{2,26},{10... | collective-permute-start | bytes 589832 | tf_op jit(solution)/shard_map/ppermute | solution.py:190
  223.0 16.2 %collective-permute-start.10 = (bf16[512,192]{1,0:T(8,128)(2,1)}, bf16[512,192]{1,0:T(8,128)(2,1)}, u32[]{:S(2)}, u32[]{:S(2)}) collective-permute-start(bf16[512,192]{1,0:T(8,128)(2,1)} %bitcast.207), channel_id=1, source_target_pairs={{0,16},{8,24},{16,0},{24,8},{1,17},{9,25},{17,1},{25,9},{2,18},{10... | collective-permute-start | bytes 589832 | tf_op jit(solution)/shard_map/ppermute | solution.py:190
  225.1 14.1 %collective-permute-start.9 = (bf16[512,192]{1,0:T(8,128)(2,1)}, bf16[512,192]{1,0:T(8,128)(2,1)}, u32[]{:S(2)}, u32[]{:S(2)}) collective-permute-start(bf16[512,192]{1,0:T(8,128)(2,1)} %bitcast.208), channel_id=1, source_target_pairs={{0,8},{8,0},{16,24},{24,16},{1,9},{9,1},{17,25},{25,17},{2,10},{10... | collective-permute-start | bytes 589832 | tf_op jit(solution)/shard_map/ppermute | solution.py:190
  236.7 2.5 copy-start.13
  280.3 14.0 %copy-start.12 = (bf16[1152,512]{1,0:T(8,128)(2,1)S(1)}, bf16[1152,512]{1,0:T(8,128)(2,1)}, u32[]{:S(2)}) copy-start(bf16[1152,512]{1,0:T(8,128)(2,1)} %copy.70) | copy-start | bytes 3538948
  280.3 14.0 %copy-start.16 = (bf16[1,512,768]{2,1,0:T(8,128)(2,1)S(1)}, bf16[1,512,768]{2,1,0:T(8,128)(2,1)}, u32[]{:S(2)}) copy-start(bf16[1,512,768]{2,1,0:T(8,128)(2,1)} %param.16) | copy-start | bytes 2359300
  293.1 13.2 %collective-permute-start.14 = (bf16[2,2,96,576]{3,2,1,0:T(8,128)(2,1)}, bf16[2,2,96,576]{3,2,1,0:T(8,128)(2,1)}, u32[]{:S(2)}, u32[]{:S(2)}) collective-permute-start(bf16[2,2,96,576]{3,2,1,0:T(8,128)(2,1)} %get-tuple-element.74), channel_id=1, source_target_pairs={{0,1},{1,0},{2,3},{3,2},{4,5},{5,4},{6,7},{7,6},{8,9},{9,8},{10,11... | collective-permute-start | bytes 1327112 | tf_op jit(solution)/shard_map/ppermute | solution.py:190
  302.8 51.0 %collective-permute-start.20 = (bf16[8,264,768]{2,1,0:T(8,128)(2,1)}, bf16[8,264,768]{2,1,0:T(8,128)(2,1)}, u32[]{:S(2)}, u32[]{:S(2)}) collective-permute-start(bf16[8,264,768]{2,1,0:T(8,128)(2,1)} %get-tuple-element.47), channel_id=1, source_target_pairs={{0,8},{8,0},{16,24},{24,16},{1,9},{9,1},{17,25},{25,17},{2,10},{10... | collective-permute-start | bytes 9732104 | tf_op jit(solution)/shard_map/ppermute | solution.py:190
  309.8 7.8 %collective-permute-start.15 = (bf16[2,96,576]{1,2,0:T(8,128)(2,1)S(1)}, bf16[2,96,576]{1,2,0:T(8,128)(2,1)S(1)}, u32[]{:S(2)}, u32[]{:S(2)}) collective-permute-start(bf16[2,96,576]{1,2,0:T(8,128)(2,1)S(1)} %dynamic-slice_bitcast_fusion.4), channel_id=1, source_target_pairs={{0,2},{1,3},{2,0},{3,1},{4,6},{5,7},{6,4},{7,5},{8,10},{9,11},{10,... | collective-permute-start | bytes 663560 | tf_op jit(solution)/shard_map/ppermute | solution.py:190
  313.3 34.1 %collective-permute-start.12 = (bf16[2,512,768]{2,1,0:T(8,128)(2,1)}, bf16[2,512,768]{2,1,0:T(8,128)(2,1)}, u32[]{:S(2)}, u32[]{:S(2)}) collective-permute-start(bf16[2,512,768]{2,1,0:T(8,128)(2,1)} %slice.122), channel_id=1, source_target_pairs={{0,8},{8,0},{16,24},{24,16},{1,9},{9,1},{17,25},{25,17},{2,10},{10... | collective-permute-start | bytes 4718600 | tf_op jit(solution)/shard_map/ppermute | solution.py:190
  317.8 9.4 %collective-permute-start.16 = (bf16[96,576]{0,1:T(8,128)(2,1)S(1)}, bf16[96,576]{0,1:T(8,128)(2,1)S(1)}, u32[]{:S(2)}, u32[]{:S(2)}) collective-permute-start(bf16[96,576]{0,1:T(8,128)(2,1)S(1)} %dynamic-slice_bitcast_fusion.15), channel_id=1, source_target_pairs={{0,4},{1,5},{2,6},{3,7},{4,0},{5,1},{6,2},{7,3},{8,12},{9,13},{10,... | collective-permute-start | bytes 331784 | tf_op jit(solution)/shard_map/ppermute | solution.py:190
  327.8 4.6 %collective-permute-start.18 = (bf16[96,576]{0,1:T(8,128)(2,1)}, bf16[96,576]{0,1:T(8,128)(2,1)}, u32[]{:S(2)}, u32[]{:S(2)}) collective-permute-start(bf16[96,576]{0,1:T(8,128)(2,1)} %fusion.37), channel_id=1, source_target_pairs={{0,16},{8,24},{16,0},{24,8},{1,17},{9,25},{17,1},{25,9},{2,18},{10... | collective-permute-start | bytes 331784 | tf_op jit(solution)/shard_map/ppermute | solution.py:190
  329.1 15.0 %collective-permute-start.17 = (bf16[96,576]{0,1:T(8,128)(2,1)}, bf16[96,576]{0,1:T(8,128)(2,1)}, u32[]{:S(2)}, u32[]{:S(2)}) collective-permute-start(bf16[96,576]{0,1:T(8,128)(2,1)} %fusion.37), channel_id=1, source_target_pairs={{0,8},{8,0},{16,24},{24,16},{1,9},{9,1},{17,25},{25,17},{2,10},{10... | collective-permute-start | bytes 331784 | tf_op jit(solution)/shard_map/ppermute | solution.py:190
  332.5 11.7 %collective-permute-start.19 = (bf16[96,576]{0,1:T(8,128)(2,1)}, bf16[96,576]{0,1:T(8,128)(2,1)}, u32[]{:S(2)}, u32[]{:S(2)}) collective-permute-start(bf16[96,576]{0,1:T(8,128)(2,1)} %collective-permute-done.18), channel_id=1, source_target_pairs={{0,8},{8,0},{16,24},{24,16},{1,9},{9,1},{17,25},{25,17},{2,10},{10... | collective-permute-start | bytes 331784 | tf_op jit(solution)/shard_map/ppermute | solution.py:190
  347.3 21.6 %copy-start.9 = (f32[96,2304]{1,0:T(8,128)}, f32[96,2304]{1,0:T(8,128)S(1)}, u32[]{:S(2)}) copy-start(f32[96,2304]{1,0:T(8,128)S(1)} %reshape.225) | copy-start | bytes 2654212
  349.9 1.8 copy-start.5
  352.6 24.6 %collective-permute-start.13 = (bf16[512,768]{1,0:T(8,128)(2,1)}, bf16[512,768]{1,0:T(8,128)(2,1)S(1)}, u32[]{:S(2)}, u32[]{:S(2)}) collective-permute-start(bf16[512,768]{1,0:T(8,128)(2,1)} %fusion.27), channel_id=1, source_target_pairs={{0,16},{8,24},{16,0},{24,8},{1,17},{9,25},{17,1},{25,9},{2,18},{10... | collective-permute-start | bytes 2359304 | tf_op jit(solution)/shard_map/ppermute | solution.py:190
  365.0 2.5 copy-start.4
  368.6 19.2 %collective-permute-start.25 = (bf16[2,2,128,2,384]{4,2,3,0,1:T(8,128)(2,1)}, bf16[2,2,128,2,384]{4,2,3,0,1:T(8,128)(2,1)}, u32[]{:S(2)}, u32[]{:S(2)}) collective-permute-start(bf16[2,2,128,2,384]{4,2,3,0,1:T(8,128)(2,1)} %bitcast.200), channel_id=1, source_target_pairs={{0,1},{1,0},{2,3},{3,2},{4,5},{5,4},{6,7},{7,6},{8,9},{9,8},{10,11... | collective-permute-start | bytes 2359304 | tf_op jit(solution)/shard_map/ppermute | solution.py:190
  370.1 1.9 slice-start
  374.1 2.6 copy-start.26
  375.6 3.7 copy-start.10
  375.6 19.9 %collective-permute-start.21 = (bf16[8,136,384]{2,1,0:T(8,128)(2,1)}, bf16[8,136,384]{2,1,0:T(8,128)(2,1)}, u32[]{:S(2)}, u32[]{:S(2)}) collective-permute-start(bf16[8,136,384]{2,1,0:T(8,128)(2,1)} %bitcast.199), channel_id=1, source_target_pairs={{0,16},{8,24},{16,0},{24,8},{1,17},{9,25},{17,1},{25,9},{2,18},{10... | collective-permute-start | bytes 2506760 | tf_op jit(solution)/shard_map/ppermute | solution.py:190
  389.4 9.6 %collective-permute-start.26 = (bf16[2,128,2,384]{3,1,2,0:T(8,128)(2,1)S(1)}, bf16[2,128,2,384]{3,1,2,0:T(8,128)(2,1)S(1)}, u32[]{:S(2)}, u32[]{:S(2)}) collective-permute-start(bf16[2,128,2,384]{3,1,2,0:T(8,128)(2,1)S(1)} %dynamic-slice_bitcast_fusion.3), channel_id=1, source_target_pairs={{0,2},{1,3},{2,0},{3,1},{4,6},{5,7},{6,4},{7,5},{8,10},{9,11},{10,... | collective-permute-start | bytes 1179656 | tf_op jit(solution)/shard_map/ppermute | solution.py:190
  396.9 9.8 %collective-permute-start.22 = (bf16[2,2,136,384]{3,2,1,0:T(8,128)(2,1)S(1)}, bf16[2,2,136,384]{3,2,1,0:T(8,128)(2,1)S(1)}, u32[]{:S(2)}, u32[]{:S(2)}) collective-permute-start(bf16[2,2,136,384]{3,2,1,0:T(8,128)(2,1)S(1)} %dynamic-slice_bitcast_fusion.2), channel_id=1, source_target_pairs={{0,1},{1,0},{2,3},{3,2},{4,5},{5,4},{6,7},{7,6},{8,9},{9,8},{10,11... | collective-permute-start | bytes 1253384 | tf_op jit(solution)/shard_map/ppermute | solution.py:190
  399.1 29.8 %copy-start.8 = (f32[512,768]{1,0:T(8,128)S(1)}, f32[512,768]{1,0:T(8,128)}, u32[]{:S(2)}) copy-start(f32[512,768]{1,0:T(8,128)} %copy-done.7) | copy-start | bytes 4718596
  399.2 29.8 %copy-start.6 = (f32[2,512,768]{2,1,0:T(8,128)S(1)}, f32[2,512,768]{2,1,0:T(8,128)}, u32[]{:S(2)}) copy-start(f32[2,512,768]{2,1,0:T(8,128)} %copy-done.5) | copy-start | bytes 9437188
  399.2 12.0 %collective-permute-start.27 = (bf16[128,2,384]{2,0,1:T(8,128)(2,1)S(1)}, bf16[128,2,384]{2,0,1:T(8,128)(2,1)S(1)}, u32[]{:S(2)}, u32[]{:S(2)}) collective-permute-start(bf16[128,2,384]{2,0,1:T(8,128)(2,1)S(1)} %dynamic-slice_bitcast_fusion.14), channel_id=1, source_target_pairs={{0,4},{1,5},{2,6},{3,7},{4,0},{5,1},{6,2},{7,3},{8,12},{9,13},{10,... | collective-permute-start | bytes 589832 | tf_op jit(solution)/shard_map/ppermute | solution.py:190
  406.8 7.8 %collective-permute-start.23 = (bf16[2,136,384]{2,1,0:T(8,128)(2,1)S(1)}, bf16[2,136,384]{2,1,0:T(8,128)(2,1)S(1)}, u32[]{:S(2)}, u32[]{:S(2)}) collective-permute-start(bf16[2,136,384]{2,1,0:T(8,128)(2,1)S(1)} %dynamic-slice_bitcast_fusion.9), channel_id=1, source_target_pairs={{0,2},{1,3},{2,0},{3,1},{4,6},{5,7},{6,4},{7,5},{8,10},{9,11},{10,... | collective-permute-start | bytes 626696 | tf_op jit(solution)/shard_map/ppermute | solution.py:190
  411.3 3.8 collective-permute-start.28
  414.7 6.6 %collective-permute-start.24 = (bf16[136,384]{1,0:T(8,128)(2,1)S(1)}, bf16[136,384]{1,0:T(8,128)(2,1)S(1)}, u32[]{:S(2)}, u32[]{:S(2)}) collective-permute-start(bf16[136,384]{1,0:T(8,128)(2,1)S(1)} %dynamic-slice_bitcast_fusion.16), channel_id=1, source_target_pairs={{0,4},{1,5},{2,6},{3,7},{4,0},{5,1},{6,2},{7,3},{8,12},{9,13},{10,... | collective-permute-start | bytes 313352 | tf_op jit(solution)/shard_map/ppermute | solution.py:190
  421.4 5.4 %collective-permute-start.30 = (bf16[264,384]{1,0:T(8,128)(2,1)S(1)}, bf16[264,384]{1,0:T(8,128)(2,1)S(1)}, u32[]{:S(2)}, u32[]{:S(2)}) collective-permute-start(bf16[264,384]{1,0:T(8,128)(2,1)S(1)} %get-tuple-element.92), channel_id=1, source_target_pairs={{0,16},{8,24},{16,0},{24,8},{1,17},{9,25},{17,1},{25,9},{2,18},{10... | collective-permute-start | bytes 608264 | tf_op jit(solution)/shard_map/ppermute | solution.py:190
  421.5 9.0 %collective-permute-start.29 = (bf16[264,384]{1,0:T(8,128)(2,1)S(1)}, bf16[264,384]{1,0:T(8,128)(2,1)S(1)}, u32[]{:S(2)}, u32[]{:S(2)}) collective-permute-start(bf16[264,384]{1,0:T(8,128)(2,1)S(1)} %get-tuple-element.92), channel_id=1, source_target_pairs={{0,8},{8,0},{16,24},{24,16},{1,9},{9,1},{17,25},{25,17},{2,10},{10... | collective-permute-start | bytes 608264 | tf_op jit(solution)/shard_map/ppermute | solution.py:190
  426.8 3.7 collective-permute-start.31
  430.6 1.7 copy-start.17
  430.7 3.2 copy-start.1
  430.8 2.7 copy-start.27
  (2 other events, 2.0 us)
Sparse Core Ops, SparseCore 0:
  10.9 57.2 all-gather.4
  71.7 55.6 all-gather.8
  130.9 60.5 all-gather.6

commit v2 on v1

v2 whole, which is shorter than its diff:
```python
import functools
import jax, jax.numpy as jnp
from jax import lax
from jax.experimental import pallas as pl
from jax.experimental.pallas import tpu as pltpu

from jax.sharding import PartitionSpec as P

HEADS = 12
HEAD = 64
PAD = 128
EPSILON = 1e-05
VMEM = 56 * 1024 * 1024
F32 = jnp.float32
BF16 = jnp.bfloat16


def _dot(a, b, ca, cb):
    return lax.dot_general(a, b, (((ca,), (cb,)), ((), ())), preferred_element_type=F32)


def _normalize(values):
    centred = values - jnp.mean(values, axis=1, keepdims=True)
    variance = jnp.mean(centred * centred, axis=1, keepdims=True)
    scale_inv = lax.rsqrt(variance + EPSILON)
    return centred * scale_inv, scale_inv


def _norm_back(grad_hat, normed, scale_inv):
    return scale_inv * (
        grad_hat
        - jnp.mean(grad_hat, axis=1, keepdims=True)
        - normed * jnp.mean(grad_hat * normed, axis=1, keepdims=True)
    )


def _half_turn(v):
    lane = lax.broadcasted_iota(jnp.int32, v.shape, 1)
    ahead = pltpu.roll(v, v.shape[1] - HEAD // 2, 1)
    behind = pltpu.roll(v, HEAD // 2, 1)
    return jnp.where(lane % HEAD < HEAD // 2, ahead, behind)


def _parts(v):
    high = v.astype(BF16)
    rest = v - high.astype(F32)
    mid = rest.astype(BF16)
    low = (rest - mid.astype(F32)).astype(BF16)
    return high, mid, low


def _with_parts(base, v):
    rows = base.shape[0]
    high, mid, low = _parts(v)
    lane = lax.broadcasted_iota(jnp.int32, (rows, PAD - HEAD), 1)
    f = lambda p: p.astype(F32)
    tail = jnp.where(lane == 0, f(high), jnp.where(lane == 1, f(mid), jnp.where(lane == 2, f(low), 0.0)))
    return jnp.concatenate([base[:, :HEAD], tail.astype(BF16)], axis=1)


def _params():
    return pltpu.CompilerParams(vmem_limit_bytes=VMEM)


def _row(block, n, first=0):
    return pl.BlockSpec((block, n), lambda i, *_: (i + first, 0))


def _whole(a):
    rank = len(a.shape)
    return pl.BlockSpec(a.shape, lambda i, *_: (0,) * rank)


def _shape(shape, dtype=BF16):
    return jax.ShapeDtypeStruct(shape, dtype)


def _cost(flops, size, transcendentals=0):
    return pl.CostEstimate(flops=int(flops), bytes_accessed=int(size), transcendentals=int(transcendentals))


def project_kernel(heads, spots, x0, x1, x2, x3, even_ref, odd_ref, cos_ref, sin_ref, w_ref, normed_ref, q_ref, k_ref, v_ref, x_scr):
    step = pl.program_id(0)
    owners = w_ref.shape[0] // even_ref.shape[1]
    share = even_ref.shape[1]

    @pl.when(step == 0)
    def _():
        for i in range(owners):
            at = slice(i * share, (i + 1) * share)
            spot = spots[i]
            if owners == 1:
                w_ref[at] = even_ref[0]
            else:
                half = owners // 2

                @pl.when(spot < half)
                def _():
                    w_ref[at] = even_ref[spot]

                @pl.when(spot >= half)
                def _():
                    w_ref[at] = odd_ref[spot - half]

    for j, ref in enumerate((x0, x1, x2, x3)):

        @pl.when(step == j)
        def _(ref=ref):
            x_scr[...] = ref[...]

    normed = _normalize(x_scr[...].astype(F32))[0].astype(BF16)
    normed_ref[...] = normed
    qkv = _dot(normed, w_ref[...], 1, 0)
    span = heads * HEAD
    qk = qkv[:, : 2 * span]
    cos = jnp.concatenate([cos_ref[...]] * heads, axis=1)
    sin = jnp.concatenate([sin_ref[...]] * heads, axis=1)
    qk = qk * cos + _half_turn(qk) * sin
    rows = x0.shape[0]
    zeros = jnp.zeros((rows, PAD - HEAD), BF16)
    ones = jnp.where(lax.broadcasted_iota(jnp.int32, (rows, PAD - HEAD), 1) < 3, 1.0, 0.0).astype(BF16)
    for h in range(heads):
        at = slice(h * PAD, (h + 1) * PAD)
        lo = h * HEAD
        q_ref[:, at] = jnp.concatenate([(qk[:, lo : lo + HEAD] * HEAD ** -0.5).astype(BF16), zeros], axis=1)
        k_ref[:, at] = jnp.concatenate([qk[:, span + lo : span + lo + HEAD].astype(BF16), ones], axis=1)
        v_ref[:, at] = jnp.concatenate([qkv[:, 2 * span + lo : 2 * span + lo + HEAD].astype(BF16), ones], axis=1)


def project(spots, xs, even, odd, cos, sin, heads):
    rows, width = xs[0].shape
    length = rows * len(xs)
    columns = even.shape[2]
    w_shape = _shape((width, columns))
    return pl.pallas_call(
        functools.partial(project_kernel, heads),
        grid_spec=pltpu.PrefetchScalarGridSpec(
            num_scalar_prefetch=1,
            grid=(len(xs),),
            in_specs=[_whole(x) for x in xs] + [_whole(even), _whole(odd), _row(rows, cos.shape[1]), _row(rows, sin.shape[1])],
            out_specs=[_whole(w_shape), _row(rows, width)] + [_row(rows, heads * PAD)] * 3,
            scratch_shapes=[pltpu.VMEM((rows, width), BF16)],
        ),
        out_shape=[w_shape, _shape((length, width))] + [_shape((length, heads * PAD))] * 3,
        compiler_params=_params(),
        cost_estimate=_cost(2 * length * width * columns, 12 << 20),
        name="project",
    )(spots, *xs, even, odd, cos, sin)


def forward_kernel(heads, q_ref, k_ref, v_ref, ctx_ref, out_ref, qx_ref):
    outs = []
    for h in range(heads):
        at = slice(h * PAD, (h + 1) * PAD)
        q = q_ref[:, at]
        scores = _dot(q, k_ref[:, at], 1, 1)
        top = jnp.max(scores, axis=1, keepdims=True)
        weights = jnp.exp(scores - top).astype(BF16)
        sums = _dot(weights, v_ref[:, at], 1, 0)
        total = sums[:, HEAD : HEAD + 1]
        outs.append(sums[:, :HEAD] / total)
        qx_ref[:, at] = _with_parts(q, -(top + jnp.log(total)))
    out = jnp.concatenate(outs, axis=1)
    out_ref[...] = out
    ctx_ref[0] = out.astype(BF16)


def attend_forward(q, k, v, heads, block, first, count):
    length = k.shape[0]
    span = heads * HEAD
    return pl.pallas_call(
        functools.partial(forward_kernel, heads),
        grid=(count,),
        in_specs=[_row(block, heads * PAD, first), _whole(k), _whole(v)],
        out_specs=[pl.BlockSpec((1, block, span), lambda i: (i, 0, 0)), _row(block, span), _row(block, heads * PAD)],
        out_shape=[_shape((count, block, span)), _shape((count * block, span), F32), _shape((count * block, heads * PAD))],
        compiler_params=_params(),
        cost_estimate=_cost(16 * heads * count * block * length * HEAD, 6 << 20, heads * count * block * length),
        name="attend_forward",
    )(q, k, v)


def backward_kernel(heads, q_ref, k_ref, v_ref, do0_ref, do1_ref, out_ref, dq_ref, dk_ref, dv_ref, dk_acc, dv_acc):
    step = pl.program_id(0)

    @pl.when(step == 0)
    def _():
        dk_acc[...] = jnp.zeros_like(dk_acc)
        dv_acc[...] = jnp.zeros_like(dv_acc)

    do_all = jnp.where(step == 0, do0_ref[...], do1_ref[...])
    prod = do_all.astype(F32) * out_ref[...]
    dqs = []
    for h in range(heads):
        at = slice(h * PAD, (h + 1) * PAD)
        lo = h * HEAD
        q, k, v = q_ref[:, at], k_ref[:, at], v_ref[:, at]
        delta = jnp.sum(prod[:, lo : lo + HEAD], axis=1, keepdims=True)
        do = _with_parts(do_all[:, lo : lo + HEAD], -delta)
        probs = jnp.exp(_dot(k, q, 1, 1))
        back = _dot(v, do, 1, 1)
        score_back = (probs * back).astype(BF16)
        dv_acc[:, at] += _dot(probs.astype(BF16), do, 1, 0)
        dk_acc[:, at] += _dot(score_back, q, 1, 0)
        dqs.append(_dot(score_back, k, 0, 0)[:, :HEAD])
    dq_ref[...] = (jnp.concatenate(dqs, axis=1) * HEAD ** -0.5).astype(BF16)

    @pl.when(step == pl.num_programs(0) - 1)
    def _():
        pick = lambda acc: jnp.concatenate([acc[:, h * PAD : h * PAD + HEAD] for h in range(heads)], axis=1).astype(BF16)
        dk_ref[...] = pick(dk_acc)
        dv_ref[...] = pick(dv_acc)


def attend_backward(q, k, v, do0, do1, out, heads):
    length = k.shape[0]
    block, span = do0.shape
    whole = _shape((length, span))
    return pl.pallas_call(
        functools.partial(backward_kernel, heads),
        grid=(2,),
        in_specs=[_row(block, heads * PAD), _whole(k), _whole(v), _whole(do0), _whole(do1), _row(block, span)],
        out_specs=[_row(block, span), _whole(whole), _whole(whole)],
        out_shape=[_shape((2 * block, span)), whole, whole],
        scratch_shapes=[pltpu.VMEM((length, heads * PAD), F32)] * 2,
        compiler_params=_params(),
        cost_estimate=_cost(40 * heads * 2 * block * length * HEAD, 8 << 20, heads * 2 * block * length),
        name="attend_backward",
    )(q, k, v, do0, do1, out)


def _gelu(first):
    cumulative = 0.5 * (1.0 + lax.erf(first * 0.5 ** 0.5))
    density = jnp.exp(-0.5 * first * first) * 0.3989422804014327
    return first * cumulative, cumulative + first * density


def feed_kernel(share, group, here, x_ref, cot_ref, own_ref, near_ref, far_ref, diag_ref, w_ref, result_ref, back_ref, grad0, grad1, grad2, ctx_ref, n2_ref, hidden_ref, gates_ref, branch_ref, attn_scr, in_scr, out_scr):
    width = x_ref.shape[1]
    hidden_size = out_scr.shape[0]
    owners = w_ref.shape[0]
    span = width // group
    blocks = in_scr.shape[0]

    @pl.when(pl.program_id(0) == 0)
    def _():
        pick = lambda lo, hi: w_ref[:, lo:hi].reshape(owners * (hi - lo), width)
        attn = pick(0, share)
        for g in range(group):
            spot = here[0] ^ g
            attn_scr[pl.ds(pl.multiple_of(spot * span, span), span)] = attn[g * span : (g + 1) * span]
        for c in range(blocks):
            in_scr[c] = pick(share * (1 + c), share * (2 + c))
        out_scr[...] = pick(share * (1 + blocks), share * (1 + blocks) + hidden_size // owners)

    ctx = jnp.concatenate([own_ref[0], near_ref[0], far_ref[0], diag_ref[0]], axis=1)
    ctx_ref[...] = ctx
    attended = x_ref[...].astype(F32) + _dot(ctx, attn_scr[...], 1, 0)
    hat, scale = _normalize(attended)
    n2 = hat.astype(BF16)
    n2_ref[...] = n2
    gate_up = jnp.concatenate([_dot(n2, in_scr[c], 1, 0) for c in range(blocks)], axis=1)
    first, second = gate_up[:, :hidden_size], gate_up[:, hidden_size:]
    gelu, slope = _gelu(first)
    hidden = (gelu * second).astype(BF16)
    hidden_ref[...] = hidden
    result_ref[0] = (attended + _dot(hidden, out_scr[...], 1, 0)).astype(BF16)
    cot = cot_ref[...]
    hidden_back = _dot(cot, out_scr[...], 1, 1)
    gates = jnp.concatenate([hidden_back * second * slope, hidden_back * gelu], axis=1).astype(BF16)
    gates_ref[...] = gates
    back = sum(_dot(gates[:, c * width : (c + 1) * width], in_scr[c], 1, 1) for c in range(blocks))
    back = cot.astype(F32) + _norm_back(back, hat, scale)
    back_ref[...] = back
    branch = back.astype(BF16)
    branch_ref[...] = branch
    grads = _dot(branch, attn_scr[...], 1, 1).astype(BF16)
    grad0[...] = grads[:, :span]
    grad1[...] = grads[:, span : 2 * span]
    grad2[0] = grads[:, 2 * span : 3 * span]
    grad2[1] = grads[:, 3 * span :]


def feed(here, x, cot, own, near, far, diag, packed, share, hidden_size, block=256):
    rows, width = x.shape
    span = own.shape[2]
    group = width // span
    blocks = 2 * hidden_size // width
    lead = lambda: pl.BlockSpec((1, block, span), lambda i, *_: (0, i, 0))
    widths = (width, width, hidden_size, 2 * hidden_size, width)
    return pl.pallas_call(
        functools.partial(feed_kernel, share, group),
        grid_spec=pltpu.PrefetchScalarGridSpec(
            num_scalar_prefetch=1,
            grid=(rows // block,),
            in_specs=[_row(block, width), _row(block, width), lead(), lead(), lead(), lead(), _whole(packed)],
            out_specs=[pl.BlockSpec((1, block, width), lambda i, *_: (0, i, 0)), _row(block, width), _row(block, span), _row(block, span), pl.BlockSpec((2, block, span), lambda i, *_: (0, i, 0))]
            + [_row(block, n) for n in widths],
            scratch_shapes=[pltpu.VMEM((width, width), BF16), pltpu.VMEM((blocks, width, width), BF16), pltpu.VMEM((hidden_size, width), BF16)],
        ),
        out_shape=[_shape((1, rows, width)), _shape((rows, width), F32), _shape((rows, span)), _shape((rows, span)), _shape((2, rows, span))]
        + [_shape((rows, n)) for n in widths],
        compiler_params=_params(),
        cost_estimate=_cost(4 * rows * width * (width + 3 * hidden_size), 20 << 20, 2 * rows * hidden_size),
        name="feed",
    )(here, x, cot, own, near, far, diag, packed)


def feed_grads_kernel(owners, share, hidden_share, group, here, ctx_ref, branch_ref, n2_ref, gates_ref, hidden_ref, cot_ref, kept_ref, sent_ref, attn_scr):
    width = branch_ref.shape[1]
    span = width // group
    half = kept_ref.shape[1]
    core = here[0] & 1

    def place(value, start, size):
        value = value.reshape(owners, size, width).astype(BF16)
        for side in range(2):
            lo, hi = max(start, side * half), min(start + size, (side + 1) * half)
            if lo < hi:
                part = value[:, lo - start : hi - start]
                at = slice(lo - side * half, hi - side * half)

                @pl.when(core == side)
                def _(part=part, at=at):
                    kept_ref[:, at] = part

                @pl.when(core != side)
                def _(part=part, at=at):
                    sent_ref[:, at] = part

    total = share * (1 + gates_ref.shape[1] // width) + hidden_share
    attn = _dot(ctx_ref[...], branch_ref[...], 0, 0)
    for g in range(group):
        spot = here[0] ^ g
        attn_scr[pl.ds(pl.multiple_of(spot * span, span), span)] = attn[g * span : (g + 1) * span]
    place(attn_scr[...], 0, share)
    n2 = n2_ref[...]
    for c in range(gates_ref.shape[1] // width):
        place(_dot(n2, gates_ref[:, c * width : (c + 1) * width], 0, 0), share * (1 + c), share)
    place(_dot(hidden_ref[...], cot_ref[...], 0, 0), total - hidden_share, hidden_share)
    if total < 2 * half:
        place(jnp.zeros((owners * (2 * half - total), width), F32), total, 2 * half - total)


def feed_grads(here, ctx, branch, n2, gates, hidden, cot, owners, half):
    width = branch.shape[1]
    arrays = (ctx, branch, n2, gates, hidden, cot)
    return pl.pallas_call(
        functools.partial(feed_grads_kernel, owners, width // owners, hidden.shape[1] // owners, 4),
        grid_spec=pltpu.PrefetchScalarGridSpec(
            num_scalar_prefetch=1,
            grid=(1,),
            in_specs=[_whole(a) for a in arrays],
            out_specs=[_whole(_shape((owners, half, width)))] * 2,
            scratch_shapes=[pltpu.VMEM((width, width), F32)],
        ),
        out_shape=[_shape((owners, half, width))] * 2,
        compiler_params=_params(),
        cost_estimate=_cost(2 * branch.shape[0] * width * (width + 3 * hidden.shape[1]), 12 << 20),
        name="feed_grads",
    )(here, *arrays)


def qkv_grads_kernel(heads, dq0, dq1, dk0, dk1, dv0, dv1, cos_ref, sin_ref, normed_ref, grads_ref, grad_ref, acc):
    step = pl.program_id(0)

    @pl.when(step == 0)
    def _():
        acc[...] = jnp.zeros_like(acc)

    cos = jnp.concatenate([cos_ref[...]] * heads, axis=1)
    sin = jnp.concatenate([sin_ref[...]] * heads, axis=1)
    dq = jnp.where(step < pl.num_programs(0) // 2, dq0[...].astype(F32), dq1[...].astype(F32))
    dk = dk0[...].astype(F32) + dk1[...].astype(F32)
    qk = jnp.concatenate([dq, dk], axis=1)
    qk = (qk * cos - _half_turn(qk) * sin).astype(BF16)
    dv = (dv0[...].astype(F32) + dv1[...].astype(F32)).astype(BF16)
    grads = jnp.concatenate([qk, dv], axis=1)
    grads_ref[...] = grads
    acc[...] += _dot(normed_ref[...], grads, 0, 0)

    @pl.when(step == pl.num_programs(0) - 1)
    def _():
        grad_ref[...] = acc[...].astype(BF16)


def qkv_grads(dqs, dks, dvs, cos, sin, normed, heads, block):
    length, width = normed.shape
    span = heads * HEAD
    grad = _shape((width, 3 * span))
    halves = length // block // 2
    return pl.pallas_call(
        functools.partial(qkv_grads_kernel, heads),
        grid=(2 * halves,),
        in_specs=[
            pl.BlockSpec((block, span), lambda i: (jnp.minimum(i, halves - 1), 0)),
            pl.BlockSpec((block, span), lambda i: (jnp.maximum(i - halves, 0), 0)),
        ]
        + [_row(block, span)] * 4
        + [_row(block, cos.shape[1])] * 2
        + [_row(block, width)],
        out_specs=[_row(block, 3 * span), _whole(grad)],
        out_shape=[_shape((length, 3 * span)), grad],
        scratch_shapes=[pltpu.VMEM(grad.shape, F32)],
        compiler_params=_params(),
        cost_estimate=_cost(2 * length * width * 3 * span, 8 << 20),
        name="qkv_grads",
    )(*dqs, *dks, *dvs, cos, sin, normed)


def input_back_kernel(grads_ref, w_ref, kept_ref, sent_ref):
    back = _dot(grads_ref[...], w_ref[...], 1, 1).astype(BF16)

    @pl.when(pl.program_id(0) % 2 == 0)
    def _():
        kept_ref[0] = back

    @pl.when(pl.program_id(0) % 2 == 1)
    def _():
        sent_ref[0] = back


def input_back(grads, w, block):
    length, columns = grads.shape
    width = w.shape[0]
    spec = pl.BlockSpec((1, block, width), lambda i: (i // 2, 0, 0))
    return pl.pallas_call(
        input_back_kernel,
        grid=(length // block,),
        in_specs=[_row(block, columns), _whole(w)],
        out_specs=[spec, spec],
        out_shape=[_shape((length // block // 2, block, width))] * 2,
        compiler_params=_params(),
        cost_estimate=_cost(2 * length * width * columns, 6 << 20),
        name="input_back",
    )(grads, w)


def exchange(value, axis, distance):
    size = lax.axis_size(axis)
    return lax.ppermute(value, axis, [(i, i ^ distance) for i in range(size)])


def gather_halves(piece, axis):
    size = lax.axis_size(axis)
    pieces, order = piece[None], [0]
    distance = size // 2
    while distance > 1:
        pieces = jnp.concatenate([pieces, exchange(pieces, axis, distance)], axis=0)
        order = order + [place ^ distance for place in order]
        distance //= 2
    other = exchange(pieces, axis, 1)
    order = order + [place ^ 1 for place in order]
    where = jnp.asarray([order.index(place) for place in range(size)], jnp.int32)
    return pieces, other, where[lax.axis_index(axis) ^ jnp.arange(size)]


def halve(addends, axis, bit, take):
    own = (lax.axis_index(axis) >> bit) & 1
    sent = sum(take(a, 1 - own).astype(F32) for a in addends).astype(BF16)
    return [take(a, own) for a in addends] + [exchange(sent, axis, 1 << bit)]


def scatter_rows(addends, axis):
    bits = lax.axis_size(axis).bit_length() - 1
    addends = [a.reshape((2,) * bits + a.shape[1:]) for a in addends]
    for bit in range(bits):
        dim = bits - 1 - bit
        addends = halve(addends, axis, bit, lambda a, at: lax.dynamic_index_in_dim(a, at, dim, keepdims=False))
    return addends


def total(addends):
    return sum(a.astype(F32) for a in addends)


ROPE_BASE = 160000.0


def rope_tables(places):
    half = HEAD // 2
    inverse = ROPE_BASE ** (-(jnp.arange(half, dtype=F32) * 2.0 / HEAD))
    angles = places[:, None] * inverse[None, :]
    cosine, sine = lax.optimization_barrier((jnp.cos(angles), jnp.sin(angles)))
    return (
        jnp.concatenate([cosine] * 4, axis=1),
        jnp.concatenate([-sine, sine] * 2, axis=1),
    )


def from_slices(block):
    far = exchange(block, "seq", 2)
    return [block, exchange(block, "seq", 1), far, exchange(far, "seq", 1)]


def in_order(blocks, here):
    stacked = jnp.stack(blocks)
    return [lax.dynamic_index_in_dim(stacked, here ^ i, 0, keepdims=False) for i in range(len(blocks))]


def up16(n):
    return -(-n // 16) * 16


def body(
    inputs,
    norm_one,
    qkv_weight,
    attn_out_weight,
    norm_two,
    mlp_in_weight,
    mlp_out_weight,
    cotangent,
):
    here = lax.axis_index("seq")
    slices = lax.axis_size("seq")
    owners = lax.axis_size("fsdp")
    heads = HEADS // slices
    span = heads * HEAD
    rows, width = inputs.shape[1:]
    share = qkv_weight.shape[0]
    hidden_share = mlp_out_weight.shape[0]
    hidden_size = hidden_share * owners
    blocks = 2 * hidden_size // width
    aligned = share % 16 == 0 and hidden_share % 16 == 0
    spot = jnp.reshape(here, (1,)).astype(jnp.int32)

    x = inputs[0]
    scaled_qkv = (qkv_weight.astype(F32) * norm_one.astype(F32)[:, None]).astype(BF16)
    scaled_in = (mlp_in_weight.astype(F32) * norm_two.astype(F32)[:, None]).astype(BF16)
    x_far = exchange(x, "seq", 2)
    own_columns = jnp.concatenate(
        [lax.dynamic_slice_in_dim(scaled_qkv, c * width + here * span, span, 1) for c in range(3)], axis=1
    )
    even, odd, spots = gather_halves(own_columns, "fsdp")
    xs = [x, exchange(x, "seq", 1), x_far, exchange(x_far, "seq", 1)]
    if not aligned:
        pieces = jnp.concatenate([even, odd], axis=0)
        even = jnp.take(pieces, spots, axis=0).reshape(1, width, 3 * span)
        odd, spots = even, jnp.zeros((1,), jnp.int32)

    shard = [attn_out_weight] + [scaled_in[:, c * width : (c + 1) * width] for c in range(blocks)] + [mlp_out_weight]
    shard_rows = share * (1 + blocks) + hidden_share
    part = up16(-(-shard_rows // slices))
    shard = jnp.concatenate(shard + [jnp.zeros((part * slices - shard_rows, width), BF16)], axis=0)
    packed = lax.all_gather(lax.dynamic_slice_in_dim(shard, here * part, part, 0), ("fsdp", "seq"), axis=0, tiled=True)
    packed = packed.reshape(owners, part * slices, width)
    packed_share = share
    if not aligned:
        cuts = [share * c for c in range(2 + blocks)] + [shard_rows]
        packed = jnp.concatenate([packed[:, a:b].reshape(-1, width) for a, b in zip(cuts, cuts[1:])], axis=0)[None]
        packed_share = width

    order = here ^ jnp.arange(slices)
    places = (order[:, None] * rows + jnp.arange(rows)[None, :]).reshape(-1).astype(F32)
    cosine, sine = rope_tables(places)

    w_qkv, normed_all, query, key, value = project(spots, xs, even, odd, cosine, sine, heads)
    context_far, out_far, query_far = attend_forward(query, key, value, heads, rows, 2, 2)
    context_far = exchange(context_far, "seq", 2)
    context_near, out_near, query_near = attend_forward(query, key, value, heads, rows, 0, 2)
    context_1 = exchange(context_near[1:], "seq", 1)
    context_3 = exchange(context_far[1:], "seq", 1)

    cot = cotangent[0]
    result, attended_grad, grad0, grad1, grad23, context_low, normed_two, hidden, gates, branch = feed(
        spot, x, cot, context_near, context_1, context_far, context_3, packed, packed_share, hidden_size
    )
    grad23 = exchange(grad23, "seq", 2)
    grad1 = exchange(grad1, "seq", 1)
    grad3 = exchange(grad23[1], "seq", 1)

    grad_rows = up16(-(-shard_rows // 2))
    packed_owners = owners if aligned else 1
    if aligned:
        kept, sent = feed_grads(spot, context_low, branch, normed_two, gates, hidden, cot, owners, grad_rows)
    else:
        whole_rows = width * (1 + blocks) + hidden_size
        kept, sent = feed_grads(spot, context_low, branch, normed_two, gates, hidden, cot, 1, whole_rows // 2)
        core = here & 1
        both = jnp.where(core == 0, jnp.concatenate([kept, sent], axis=1), jnp.concatenate([sent, kept], axis=1))[0]
        cuts = [width * c for c in range(2 + blocks)] + [whole_rows]
        both = jnp.concatenate([both[a:b].reshape(owners, -1, width) for a, b in zip(cuts, cuts[1:])], axis=1)
        both = jnp.pad(both, ((0, 0), (0, 2 * grad_rows - shard_rows), (0, 0)))
        kept = lax.dynamic_slice_in_dim(both, core * grad_rows, grad_rows, 1)
        sent = lax.dynamic_slice_in_dim(both, (1 - core) * grad_rows, grad_rows, 1)
    mlp_grads = [kept, exchange(sent, "seq", 1)]
    cut = up16(grad_rows // 2)
    columns = lambda a, at: lax.dynamic_slice_in_dim(a, at * (width // 2), width // 2, a.ndim - 1)
    one = scatter_rows(halve([a[:, :cut] for a in mlp_grads], "seq", 1, columns), "fsdp")
    two = halve(scatter_rows([a[:, cut:] for a in mlp_grads], "fsdp"), "seq", 1, columns)
    mlp_part = jnp.concatenate([total(one), total(two)], axis=0).astype(BF16)

    dq_near, dk_near, dv_near = attend_backward(query_near, key, value, grad0, grad1, out_near, heads)
    dq_far, dk_far, dv_far = attend_backward(query_far, key, value, grad23[0], grad3, out_far, heads)
    qkv_back, qkv_grad = qkv_grads(
        (dq_near, dq_far), (dk_near, dk_far), (dv_near, dv_far), cosine, sine, normed_all, heads, rows
    )
    qkv_part = total(scatter_rows([qkv_grad.reshape(owners, share, 3 * span)], "fsdp")).astype(BF16)

    back_kept, back_sent = input_back(qkv_back, w_qkv, rows)
    back_near = exchange(back_sent, "seq", 1)
    back_far = exchange((back_kept[1].astype(F32) + back_near[1].astype(F32)).astype(BF16), "seq", 2)
    normed_hat, scale_inv = _normalize(x.astype(F32))
    input_grad = attended_grad + _norm_back(total([back_kept[0], back_near[0], back_far]), normed_hat, scale_inv)

    qkv_blocks = in_order(from_slices(qkv_part), here)
    qkv_sum = jnp.concatenate(
        [b[:, c * span : (c + 1) * span] for c in range(3) for b in qkv_blocks], axis=1
    ).astype(F32)

    mlp_blocks = in_order(from_slices(mlp_part), here)
    mlp_sum = jnp.concatenate(
        [jnp.concatenate([mlp_blocks[core], mlp_blocks[2 + core]], axis=1) for core in range(2)], axis=0
    ).astype(F32)
    in_sum = jnp.concatenate([mlp_sum[share * (1 + c) : share * (2 + c)] for c in range(blocks)], axis=1)
    first_out = share * (1 + blocks)
    return (
        result,
        input_grad.astype(BF16)[None],
        jnp.sum(qkv_weight.astype(F32) * qkv_sum, axis=1),
        qkv_sum * norm_one.astype(F32)[:, None],
        mlp_sum[:share],
        jnp.sum(mlp_in_weight.astype(F32) * in_sum, axis=1),
        in_sum * norm_two.astype(F32)[:, None],
        mlp_sum[first_out : first_out + hidden_share],
    )


def solution(mesh):
    tokens = P("fsdp", "seq", None)
    vector = P("fsdp")
    matrix = P("fsdp", None)
    return jax.shard_map(
        body,
        mesh=mesh,
        in_specs=(tokens, vector, matrix, matrix, vector, matrix, matrix, tokens),
        out_specs=(tokens, tokens, vector, matrix, matrix, vector, matrix, matrix),
        check_vma=False,
    )
```

time: 447 us -> 325 us (0.73)
  local copies, waits for them, and re-layouts: 93.6 us -> 19.9 us
  Pallas kernels: 82.3 us -> 126 us
  waiting for transfers between devices: 129 us -> 87.2 us
  matrix products: 28.8 us -> 0 us
  between operations: 30.5 us -> 14.9 us
  other arithmetic: 45.9 us -> 37.2 us
    all_gather x3 -> x1, waiting for transfers between devices: 55.7 us -> 0.01 us  [body(): lax.all_gather(lax.dynamic_slice_in_dim(shard, here * part, part, 0), ('f...]
    pallas_call x4 -> x9, Pallas kernels: 82.3 us -> 126 us  [the longest x2 43.4 us: attend_backward(): pl.pallas_call(functools.partial(backward_kernel, heads), grid=(2,), in_s...]
    dot_general x9 -> x0, matrix products: 28.8 us -> none  [the longest x6 18.5 us: _dot(): lax.dot_general(a, b, (((ca,), (cb,)), ((), ())), preferred_element_type=...]
    unnamed x73 -> x54, local copies, waits for them, and re-layouts: 30.3 us -> 3.6 us
    dynamic_slice x14 -> x4, local copies, waits for them, and re-layouts: 25.6 us -> 1.02 us  [the longest x1 0.71 us: body(): lax.dynamic_slice_in_dim(shard, here * part, part, 0)]
    ppermute x32, waiting for transfers between devices: 72.8 us -> 87.2 us  [exchange(): return lax.ppermute(value, axis, [(i, i ^ distance) for i in range(size)])]
    ppermute x4 -> x0, local copies, waits for them, and re-layouts: 8.82 us -> none  [exchange(): return lax.ppermute(value, axis, [(i, i ^ distance) for i in range(size)])]
    concatenate x6 -> x3, other arithmetic: 8.49 us -> 1.17 us  [the longest x2 1.15 us: gather_halves(): pieces = jnp.concatenate([pieces, exchange(pieces, axis, distance)], axis=0)]
  transfers between devices with their start and end apart: 35 -> 33, of which waited for: 18 -> 17; matrix products, arithmetic and copies ran while one was open for 29% -> 15% of each run, Pallas kernels for 7% -> 34%
where the time goes in v2:
time: 325 us; the launch traced here: 319 us
  Pallas kernels  126 us (39%)
  waiting for transfers between devices  87.2 us (27%)
  other arithmetic  37.2 us (11%)
  starting transfers between devices  34.3 us (11%)
  local copies, waits for them, and re-layouts  19.9 us (6%)
  between operations  14.9 us (5%)
    ppermute x32, waiting for transfers between devices, exchange(): return lax.ppermute(value, axis, [(i, i ^ distance) for i in range(size)])  87.2 us
    pallas_call x2, Pallas kernels, attend_backward(): pl.pallas_call(functools.partial(backward_kernel, heads), grid=(2,), in_s...  43.4 us
    ppermute x32, starting transfers between devices, exchange(): return lax.ppermute(value, axis, [(i, i ^ distance) for i in range(size)])  34.3 us
    pallas_call x2, Pallas kernels, attend_forward(): pl.pallas_call(functools.partial(forward_kernel, heads), grid=(count,), i...  27.1 us
    pallas_call x1, Pallas kernels, feed(): pl.pallas_call(functools.partial(feed_kernel, share, group), grid_spec=pl...  16.3 us
    pallas_call x1, Pallas kernels, feed_grads(): pl.pallas_call(functools.partial(feed_grads_kernel, owners, width // owne...  11.5 us
    pallas_call x1, Pallas kernels, project(): pl.pallas_call(functools.partial(project_kernel, heads), grid_spec=pltpu....  11 us
    pallas_call x1, Pallas kernels, qkv_grads(): pl.pallas_call(functools.partial(qkv_grads_kernel, heads), grid=(2 * halv...  9.18 us
  transfers between devices with their start and end apart: 33, of which 17 were waited for; matrix products, arithmetic and copies ran while one was open for 15% of the time, Pallas kernels for 34%

profile of v2, /device:TPU:1, one launch (start us, length us, event | category | flops | bytes accessed | tf_op | source)
XLA Modules:
  0.0 319.2 jit_solution(9858896964430927666)
XLA Ops:
  9.0 1.2 fusion.11
  11.0 2.1 collective-permute-start.1
  14.4 2.4 collective-permute-start.3
  16.9 6.1 %collective-permute-done.3 = bf16[1,96,576]{2,1,0:T(8,128)(2,1)S(1)} collective-permute-done((bf16[1,96,576]{2,1,0:T(8,128)(2,1)S(1)}, bf16[1,96,576]{2,1,0:T(8,128)(2,1)S(1)}, u32[]{:S(2)}, u32[]{:S(2)}) %collective-permute-start.3) | collective-permute-done | bytes 110624 | tf_op jit(solution)/shard_map/ppermute | solution.py:441
  23.8 8.2 %collective-permute-done.1.x2 = bf16[512,768]{1,0:T(8,128)(2,1)} collective-permute-done((bf16[512,768]{1,0:T(8,128)(2,1)S(1)}, bf16[512,768]{1,0:T(8,128)(2,1)}, u32[]{:S(2)}, u32[]{:S(2)}) %collective-permute-start.1) | collective-permute-done | bytes 786464 | tf_op jit(solution)/shard_map/ppermute | solution.py:441
  32.1 1.2 collective-permute-start.2
  33.3 3.7 %multiply_sine_fusion = (f32[2048,32]{1,0:T(8,128)S(1)}, f32[2048,32]{1,0:T(8,128)S(1)}) fusion(f32[32]{0:T(128)S(1)} %negate_power_fusion, f32[2048]{0:T(1024)S(1)} %bitcast.181), kind=kLoop, calls=%fused_computation.17 | loop fusion | flops 65536 | bytes 532608 | tf_op jit(solution)/shard_map/sin | solution.py:484
  37.0 1.1 pad_maximum_fusion.4.even_ref
  38.1 1.5 collective-permute-start.5
  39.6 1.1 neg.11
  40.8 1.2 gather_fusion
  41.9 4.7 %pad_maximum_fusion = (f32[2048,128]{1,0:T(8,128)}, f32[2048,128]{1,0:T(8,128)}) fusion(f32[2048,32]{1,0:T(8,128)S(1)} %get-tuple-element.43, f32[2048,32]{1,0:T(8,128)S(1)} %get-tuple-element.44, f32[2048,32]{1,0:T(8,128)} %neg.11), kind=kLoop, calls=%fused_computation.24 | loop fusion | flops 1572864 | bytes 2883584 | tf_op jit(solution)/shard_map/concatenate | solution.py:486
  46.6 10.9 %collective-permute-done.5.odd_ref = bf16[4,96,576]{2,1,0:T(8,128)(2,1)} collective-permute-done((bf16[4,96,576]{2,1,0:T(8,128)(2,1)S(1)}, bf16[4,96,576]{2,1,0:T(8,128)(2,1)}, u32[]{:S(2)}, u32[]{:S(2)}) %collective-permute-start.5) | collective-permute-done | bytes 442400 | tf_op jit(solution)/shard_map/ppermute | solution.py:441
  57.5 11.0 %project.1 = (bf16[768,576]{1,0:T(8,128)(2,1)}, bf16[2048,768]{1,0:T(8,128)(2,1)}, bf16[2048,384]{1,0:T(8,128)(2,1)}, bf16[2048,384]{1,0:T(8,128)(2,1)}, bf16[2048,384]{1,0:T(8,128)(2,1)}) custom-call(s32[8]{0:T(128)} %gather_fusion, bf16[512,768]{1,0:T(8,128)(2,1)} %bitcast.146, bf16[512,768]{1,0:T(8,128)(2,1)} %collective-permute-done.x1, ...), custom_call_target="tpu_custom_call" | custom-call | flops 1811939328 | bytes 12582912 | tf_op jit(solution)/shard_map/project/pallas_call | solution.py:135
  68.5 13.4 %attend_forward.3 = (bf16[2,512,192]{2,1,0:T(8,128)(2,1)}, f32[1024,192]{1,0:T(8,128)}, bf16[1024,384]{1,0:T(8,128)(2,1)}) custom-call(bf16[2048,384]{1,0:T(8,128)(2,1)} %get-tuple-element.45.q_ref, bf16[2048,384]{1,0:T(8,128)(2,1)} %get-tuple-element.46.k_ref, bf16[2048,384]{1,0:T(8,128)(2,1)} %get-tuple-element.47.v_ref), custom_call_target="tpu_custom_call" | custom-call | flops 6442450944 | bytes 6291456 | tf_op jit(solution)/shard_map/attend_forward/pallas_call | solution.py:171
  81.9 1.5 collective-permute-start.7
  83.3 13.7 %attend_forward.2 = (bf16[2,512,192]{2,1,0:T(8,128)(2,1)}, f32[1024,192]{1,0:T(8,128)}, bf16[1024,384]{1,0:T(8,128)(2,1)}) custom-call(bf16[2048,384]{1,0:T(8,128)(2,1)} %get-tuple-element.45.q_ref, bf16[2048,384]{1,0:T(8,128)(2,1)} %get-tuple-element.46.k_ref, bf16[2048,384]{1,0:T(8,128)(2,1)} %get-tuple-element.47.v_ref), custom_call_target="tpu_custom_call" | custom-call | flops 6442450944 | bytes 6291456 | tf_op jit(solution)/shard_map/attend_forward/pallas_call | solution.py:171
  101.2 16.3 %feed.1 = (bf16[1,512,768]{2,1,0:T(8,128)(2,1)}, f32[512,768]{1,0:T(8,128)}, bf16[512,192]{1,0:T(8,128)(2,1)}, bf16[512,192]{1,0:T(8,128)(2,1)}, bf16[2,512,192]...) custom-call(s32[1]{0:T(128)} %bitcast.here, ...), custom_call_target="tpu_custom_call" | custom-call | flops 6643777536 | bytes 20971520 | tf_op jit(solution)/shard_map/feed/pallas_call | solution.py:291
  117.7 11.5 %feed_grads.1 = (bf16[8,272,768]{2,1,0:T(8,128)(2,1)}, bf16[8,272,768]{2,1,0:T(8,128)(2,1)}) custom-call(s32[1]{0:T(128)} %bitcast.here, bf16[512,768]{1,0:T(8,128)(2,1)} %get-tuple-element.71.ctx_ref, bf16[512,768]{1,0:T(8,128)(2,1)} %get-tuple-element.72.branch_ref, bf16[512,768]{1,0:T(8,128)(2,1)} %get-tuple-element.73.n2_ref, ...), custom_call_target="tpu_custom_call" | custom-call | flops 3321888768 | bytes 12582912 | tf_op jit(solution)/shard_map/feed_grads/pallas_call | solution.py:348
  129.8 1.2 collective-permute-done.10
  131.8 1.1 collective-permute-start.11
  132.9 2.7 collective-permute-done.9.do1_ref
  136.3 21.7 %attend_backward.2 = (bf16[1024,192]{1,0:T(8,128)(2,1)}, bf16[2048,192]{1,0:T(8,128)(2,1)}, bf16[2048,192]{1,0:T(8,128)(2,1)}) custom-call(bf16[1024,384]{1,0:T(8,128)(2,1)} %get-tuple-element.52.q_ref, bf16[2048,384]{1,0:T(8,128)(2,1)} %get-tuple-element.46.k_ref, bf16[2048,384]{1,0:T(8,128)(2,1)} %get-tuple-element.47.v_ref, ...), custom_call_target="tpu_custom_call" | custom-call | flops 16106127360 | bytes 8388608 | tf_op jit(solution)/shard_map/attend_backward/pallas_call | solution.py:219
  158.6 21.7 %attend_backward.3 = (bf16[1024,192]{1,0:T(8,128)(2,1)}, bf16[2048,192]{1,0:T(8,128)(2,1)}, bf16[2048,192]{1,0:T(8,128)(2,1)}) custom-call(bf16[1024,384]{1,0:T(8,128)(2,1)} %get-tuple-element.57.q_ref, bf16[2048,384]{1,0:T(8,128)(2,1)} %get-tuple-element.46.k_ref, bf16[2048,384]{1,0:T(8,128)(2,1)} %get-tuple-element.47.v_ref, ...), custom_call_target="tpu_custom_call" | custom-call | flops 16106127360 | bytes 8388608 | tf_op jit(solution)/shard_map/attend_backward/pallas_call | solution.py:219
  180.4 9.2 %qkv_grads.1 = (bf16[2048,576]{1,0:T(8,128)(2,1)}, bf16[768,576]{1,0:T(8,128)(2,1)}) custom-call(bf16[1024,192]{1,0:T(8,128)(2,1)} %get-tuple-element.56.dq0, bf16[1024,192]{1,0:T(8,128)(2,1)} %get-tuple-element.60.dq1, bf16[2048,192]{1,0:T(8,128)(2,1)} %get-tuple-element.61.dk0, bf16[2048,192]{1,0:T(8,128)(2,1)} %get-tuple-element.62.dk1, ...), custom_call_target="tpu_custom_call" | custom-call | flops 1811939328 | bytes 8388608 | tf_op jit(solution)/shard_map/qkv_grads/pallas_call | solution.py:392
  189.6 1.2 copy_bitcast_fusion
  190.7 1.5 collective-permute-start.14
  192.4 11.1 %collective-permute-done.14 = bf16[2,2,96,576]{3,2,0,1:T(8,128)(2,1)S(1)} collective-permute-done((bf16[2,2,96,576]{3,2,0,1:T(8,128)(2,1)S(1)}, bf16[2,2,96,576]{3,2,0,1:T(8,128)(2,1)S(1)}, u32[]{:S(2)}, u32[]{:S(2)}) %collective-permute-start.14) | collective-permute-done | bytes 442400 | tf_op jit(solution)/shard_map/ppermute | solution.py:441
  203.6 1.6 collective-permute-start.15
  205.5 4.8 %collective-permute-done.15 = bf16[2,96,576]{2,1,0:T(8,128)(2,1)S(1)} collective-permute-done((bf16[2,96,576]{2,1,0:T(8,128)(2,1)S(1)}, bf16[2,96,576]{2,1,0:T(8,128)(2,1)S(1)}, u32[]{:S(2)}, u32[]{:S(2)}) %collective-permute-start.15) | collective-permute-done | bytes 221216 | tf_op jit(solution)/shard_map/ppermute | solution.py:441
  210.3 2.5 collective-permute-start.16
  212.9 7.2 %input_back.1 = (bf16[2,512,768]{2,1,0:T(8,128)(2,1)}, bf16[2,512,768]{2,1,0:T(8,128)(2,1)}) custom-call(bf16[2048,576]{1,0:T(8,128)(2,1)} %get-tuple-element.66.grads_ref, bf16[768,576]{1,0:T(8,128)(2,1)} %get-tuple-element.67.w_ref), custom_call_target="tpu_custom_call" | custom-call | flops 1811939328 | bytes 6291456 | tf_op jit(solution)/shard_map/input_back/pallas_call | solution.py:427
  220.0 2.1 collective-permute-start.12
  222.3 1.1 collective-permute-start.18
  223.4 1.6 slice.119
  225.0 1.5 slice.121
  230.6 1.6 slice.150
  232.2 1.1 add_convert_fusion
  234.4 1.5 slice.151
  235.9 1.1 fusion.15
  237.4 1.2 collective-permute-start.25
  239.3 2.2 fusion.14
  242.4 2.0 concatenate.58
  244.5 11.6 %collective-permute-done.25 = bf16[2,2,128,768]{3,2,1,0:T(8,128)(2,1)} collective-permute-done((bf16[2,2,128,768]{3,2,1,0:T(8,128)(2,1)}, bf16[2,2,128,768]{3,2,1,0:T(8,128)(2,1)}, u32[]{:S(2)}, u32[]{:S(2)}) %collective-permute-start.25) | collective-permute-done | bytes 786464 | tf_op jit(solution)/shard_map/ppermute | solution.py:441
  256.1 1.3 fusion.17
  257.4 1.3 collective-permute-start.26
  258.8 1.2 fusion.20
  260.0 1.3 collective-permute-start.22
  261.3 1.7 convert_multiply_fusion
  263.0 8.3 %collective-permute-done.13 = bf16[512,768]{1,0:T(8,128)(2,1)} collective-permute-done((bf16[512,768]{1,0:T(8,128)(2,1)}, bf16[512,768]{1,0:T(8,128)(2,1)}, u32[]{:S(2)}, u32[]{:S(2)}) %collective-permute-start.13) | collective-permute-done | bytes 786464 | tf_op jit(solution)/shard_map/ppermute | solution.py:441
  271.3 2.1 fusion.36
  273.4 1.1 fusion.22
  275.7 1.3 collective-permute-start.23
  277.1 8.5 %collective-permute-done.27 = bf16[128,768]{1,0:T(8,128)(2,1)S(1)} collective-permute-done((bf16[128,768]{1,0:T(8,128)(2,1)S(1)}, bf16[128,768]{1,0:T(8,128)(2,1)S(1)}, u32[]{:S(2)}, u32[]{:S(2)}) %collective-permute-start.27) | collective-permute-done | bytes 196640 | tf_op jit(solution)/shard_map/ppermute | solution.py:441
  285.6 1.1 fusion.32
  286.7 1.1 collective-permute-start.28
  288.9 1.3 collective-permute-done.28
  290.2 1.2 fusion.35
  291.4 5.3 %collective-permute-done.24 = bf16[144,384]{1,0:T(8,128)(2,1)S(1)} collective-permute-done((bf16[144,384]{1,0:T(8,128)(2,1)S(1)}, bf16[144,384]{1,0:T(8,128)(2,1)S(1)}, u32[]{:S(2)}, u32[]{:S(2)}) %collective-permute-start.24) | collective-permute-done | bytes 110624 | tf_op jit(solution)/shard_map/ppermute | solution.py:441
  298.1 1.3 collective-permute-start.29
  299.4 4.4 %collective-permute-done.30 = bf16[272,384]{1,0:T(8,128)(2,1)S(1)} collective-permute-done((bf16[272,384]{1,0:T(8,128)(2,1)S(1)}, bf16[272,384]{1,0:T(8,128)(2,1)S(1)}, u32[]{:S(2)}, u32[]{:S(2)}) %collective-permute-start.30) | collective-permute-done | bytes 208928 | tf_op jit(solution)/shard_map/ppermute | solution.py:441
  303.8 1.5 collective-permute-start.31
  305.4 3.0 fusion.16
  310.2 1.7 fusion.18
  (132 shorter events, 25.4 us)
Async XLA Ops:
  7.2 3.0 copy-start.16
  7.2 93.3 %all-gather.2.cloned.1.call-start = ((), (), s32[]{:S(2)}) async-start(), calls=%async_computation | async-start | bytes 7299072 | tf_op jit(solution)/shard_map/all_gather | solution.py:546
  7.9 3.0 copy-start.1
  7.9 6.1 %copy-start.23 = (bf16[96]{0:T(256)(128)(2,1)S(1)}, bf16[96]{0:T(256)(128)(2,1)}, u32[]{:S(2)}) copy-start(bf16[96]{0:T(256)(128)(2,1)} %param.10) | copy-start | bytes 580
  7.9 6.1 %copy-start.8 = (bf16[96,2304]{1,0:T(8,128)(2,1)S(1)}, bf16[96,2304]{1,0:T(8,128)(2,1)}, u32[]{:S(2)}) copy-start(bf16[96,2304]{1,0:T(8,128)(2,1)} %param.11) | copy-start | bytes 1327108
  11.0 21.1 %collective-permute-start.1 = (bf16[512,768]{1,0:T(8,128)(2,1)S(1)}, bf16[512,768]{1,0:T(8,128)(2,1)}, u32[]{:S(2)}, u32[]{:S(2)}) collective-permute-start(bf16[512,768]{1,0:T(8,128)(2,1)S(1)} %bitcast.148), channel_id=1, source_target_pairs={{0,16},{8,24},{16,0},{24,8},{1,17},{9,25},{17,1},{25,9},{2,18},{10... | collective-permute-start | bytes 2359304 | tf_op jit(solution)/shard_map/ppermute | solution.py:441
  13.1 44.4 %collective-permute-start = (bf16[512,768]{1,0:T(8,128)(2,1)S(1)}, bf16[512,768]{1,0:T(8,128)(2,1)}, u32[]{:S(2)}, u32[]{:S(2)}) collective-permute-start(bf16[512,768]{1,0:T(8,128)(2,1)S(1)} %bitcast.149), channel_id=1, source_target_pairs={{0,8},{8,0},{16,24},{24,16},{1,9},{9,1},{17,25},{25,17},{2,10},{10... | collective-permute-start | bytes 2359304 | tf_op jit(solution)/shard_map/ppermute | solution.py:441
  14.4 8.5 %collective-permute-start.3 = (bf16[1,96,576]{2,1,0:T(8,128)(2,1)S(1)}, bf16[1,96,576]{2,1,0:T(8,128)(2,1)S(1)}, u32[]{:S(2)}, u32[]{:S(2)}) collective-permute-start(bf16[1,96,576]{2,1,0:T(8,128)(2,1)S(1)} %maximum_bitcast_fusion), channel_id=1, source_target_pairs={{0,4},{1,5},{2,6},{3,7},{4,0},{5,1},{6,2},{7,3},{8,12},{9,13},{10,... | collective-permute-start | bytes 331784 | tf_op jit(solution)/shard_map/ppermute | solution.py:441
  23.0 10.3 %copy-start.15 = (bf16[1,96,576]{2,1,0:T(8,128)(2,1)}, bf16[1,96,576]{2,1,0:T(8,128)(2,1)S(1)}, u32[]{:S(2)}) copy-start(bf16[1,96,576]{2,1,0:T(8,128)(2,1)S(1)} %collective-permute-done.3) | copy-start | bytes 331780
  23.0 14.0 %collective-permute-start.4 = (bf16[2,96,576]{2,1,0:T(8,128)(2,1)S(1)}, bf16[2,96,576]{2,1,0:T(8,128)(2,1)}, u32[]{:S(2)}, u32[]{:S(2)}) collective-permute-start(bf16[2,96,576]{2,1,0:T(8,128)(2,1)S(1)} %pad_maximum_fusion.6), channel_id=1, source_target_pairs={{0,2},{1,3},{2,0},{3,1},{4,6},{5,7},{6,4},{7,5},{8,10},{9,11},{10,... | collective-permute-start | bytes 663560 | tf_op jit(solution)/shard_map/ppermute | solution.py:441
  32.1 25.4 %collective-permute-start.2 = (bf16[512,768]{1,0:T(8,128)(2,1)}, bf16[512,768]{1,0:T(8,128)(2,1)}, u32[]{:S(2)}, u32[]{:S(2)}) collective-permute-start(bf16[512,768]{1,0:T(8,128)(2,1)} %collective-permute-done.1.x2), channel_id=1, source_target_pairs={{0,8},{8,0},{16,24},{24,16},{1,9},{9,1},{17,25},{25,17},{2,10},{10... | collective-permute-start | bytes 2359304 | tf_op jit(solution)/shard_map/ppermute | solution.py:441
  37.0 3.8 %copy-start = (s32[8]{0:T(128)S(1)}, s32[8]{0:T(128)}, u32[]{:S(2)}) copy-start(s32[8]{0:T(128)} %constant.1102.clone) | copy-start | bytes 100
  38.1 8.5 %copy-start.14 = (bf16[4,96,576]{2,1,0:T(8,128)(2,1)}, bf16[4,96,576]{2,1,0:T(8,128)(2,1)S(1)}, u32[]{:S(2)}) copy-start(bf16[4,96,576]{2,1,0:T(8,128)(2,1)S(1)} %pad_maximum_fusion.4.even_ref) | copy-start | bytes 1327108
  38.1 19.3 %collective-permute-start.5 = (bf16[4,96,576]{2,1,0:T(8,128)(2,1)S(1)}, bf16[4,96,576]{2,1,0:T(8,128)(2,1)}, u32[]{:S(2)}, u32[]{:S(2)}) collective-permute-start(bf16[4,96,576]{2,1,0:T(8,128)(2,1)S(1)} %pad_maximum_fusion.4.even_ref), channel_id=1, source_target_pairs={{0,1},{1,0},{2,3},{3,2},{4,5},{5,4},{6,7},{7,6},{8,9},{9,8},{10,11... | collective-permute-start | bytes 1327112 | tf_op jit(solution)/shard_map/ppermute | solution.py:441
  81.9 17.0 %collective-permute-start.7 = (bf16[2,512,192]{2,1,0:T(8,128)(2,1)}, bf16[2,512,192]{2,1,0:T(8,128)(2,1)S(1)}, u32[]{:S(2)}, u32[]{:S(2)}) collective-permute-start(bf16[2,512,192]{2,1,0:T(8,128)(2,1)} %get-tuple-element.49), channel_id=1, source_target_pairs={{0,16},{8,24},{16,0},{24,8},{1,17},{9,25},{17,1},{25,9},{2,18},{10... | collective-permute-start | bytes 1179656 | tf_op jit(solution)/shard_map/ppermute | solution.py:441
  98.0 2.1 collective-permute-start.6
  98.9 1.6 copy-start.17
  98.9 1.6 collective-permute-start.8
  100.0 0.7 copy-start.19
  100.5 0.7 copy-start.21
  117.5 13.5 %collective-permute-start.10 = (bf16[2,512,192]{2,1,0:T(8,128)(2,1)}, bf16[2,512,192]{2,1,0:T(8,128)(2,1)S(1)}, u32[]{:S(2)}, u32[]{:S(2)}) collective-permute-start(bf16[2,512,192]{2,1,0:T(8,128)(2,1)} %get-tuple-element.58), channel_id=1, source_target_pairs={{0,16},{8,24},{16,0},{24,8},{1,17},{9,25},{17,1},{25,9},{2,18},{10... | collective-permute-start | bytes 1179656 | tf_op jit(solution)/shard_map/ppermute | solution.py:441
  117.7 12.1 %copy-start.18 = (bf16[512,192]{1,0:T(8,128)(2,1)S(1)}, bf16[512,192]{1,0:T(8,128)(2,1)}, u32[]{:S(2)}) copy-start(bf16[512,192]{1,0:T(8,128)(2,1)} %get-tuple-element.54) | copy-start | bytes 589828
  129.2 101.4 %collective-permute-start.20 = (bf16[8,272,768]{2,1,0:T(8,128)(2,1)}, bf16[8,272,768]{2,1,0:T(8,128)(2,1)}, u32[]{:S(2)}, u32[]{:S(2)}) collective-permute-start(bf16[8,272,768]{2,1,0:T(8,128)(2,1)} %get-tuple-element.77), channel_id=1, source_target_pairs={{0,8},{8,0},{16,24},{24,16},{1,9},{9,1},{17,25},{25,17},{2,10},{10... | collective-permute-start | bytes 10027016 | tf_op jit(solution)/shard_map/ppermute | solution.py:441
  129.7 5.8 %collective-permute-start.9 = (bf16[512,192]{1,0:T(8,128)(2,1)S(1)}, bf16[512,192]{1,0:T(8,128)(2,1)S(1)}, u32[]{:S(2)}, u32[]{:S(2)}) collective-permute-start(bf16[512,192]{1,0:T(8,128)(2,1)S(1)} %copy-done.18), channel_id=1, source_target_pairs={{0,8},{8,0},{16,24},{24,16},{1,9},{9,1},{17,25},{25,17},{2,10},{10... | collective-permute-start | bytes 589832 | tf_op jit(solution)/shard_map/ppermute | solution.py:441
  131.8 26.1 %collective-permute-start.11 = (bf16[512,192]{1,0:T(8,128)(2,1)S(1)}, bf16[512,192]{1,0:T(8,128)(2,1)S(1)}, u32[]{:S(2)}, u32[]{:S(2)}) collective-permute-start(bf16[512,192]{1,0:T(8,128)(2,1)S(1)} %get-tuple-element.90), channel_id=1, source_target_pairs={{0,8},{8,0},{16,24},{24,16},{1,9},{9,1},{17,25},{25,17},{2,10},{10... | collective-permute-start | bytes 589832 | tf_op jit(solution)/shard_map/ppermute | solution.py:441
  135.5 0.7 copy-start.22
  157.9 0.7 copy-start.20
  180.4 11.9 %copy-start.2 = (bf16[1,512,768]{2,1,0:T(8,128)(2,1)S(1)}, bf16[1,512,768]{2,1,0:T(8,128)(2,1)}, u32[]{:S(2)}) copy-start(bf16[1,512,768]{2,1,0:T(8,128)(2,1)} %param.9) | copy-start | bytes 2359300
  189.6 13.9 %copy-start.13 = (bf16[768,576]{1,0:T(8,128)(2,1)S(1)}, bf16[768,576]{1,0:T(8,128)(2,1)}, u32[]{:S(2)}) copy-start(bf16[768,576]{1,0:T(8,128)(2,1)} %get-tuple-element.70) | copy-start | bytes 2654212
  190.7 12.8 %collective-permute-start.14 = (bf16[2,2,96,576]{3,2,0,1:T(8,128)(2,1)S(1)}, bf16[2,2,96,576]{3,2,0,1:T(8,128)(2,1)S(1)}, u32[]{:S(2)}, u32[]{:S(2)}) collective-permute-start(bf16[2,2,96,576]{3,2,0,1:T(8,128)(2,1)S(1)} %copy_bitcast_fusion), channel_id=1, source_target_pairs={{0,1},{1,0},{2,3},{3,2},{4,5},{5,4},{6,7},{7,6},{8,9},{9,8},{10,11... | collective-permute-start | bytes 1327112 | tf_op jit(solution)/shard_map/ppermute | solution.py:441
  203.6 6.7 %collective-permute-start.15 = (bf16[2,96,576]{2,1,0:T(8,128)(2,1)S(1)}, bf16[2,96,576]{2,1,0:T(8,128)(2,1)S(1)}, u32[]{:S(2)}, u32[]{:S(2)}) collective-permute-start(bf16[2,96,576]{2,1,0:T(8,128)(2,1)S(1)} %fusion.19), channel_id=1, source_target_pairs={{0,2},{1,3},{2,0},{3,1},{4,6},{5,7},{6,4},{7,5},{8,10},{9,11},{10,... | collective-permute-start | bytes 663560 | tf_op jit(solution)/shard_map/ppermute | solution.py:441
  210.3 11.8 %collective-permute-start.16 = (bf16[96,576]{1,0:T(8,128)(2,1)S(1)}, bf16[96,576]{1,0:T(8,128)(2,1)S(1)}, u32[]{:S(2)}, u32[]{:S(2)}) collective-permute-start(bf16[96,576]{1,0:T(8,128)(2,1)S(1)} %fusion.23), channel_id=1, source_target_pairs={{0,4},{1,5},{2,6},{3,7},{4,0},{5,1},{6,2},{7,3},{8,12},{9,13},{10,... | collective-permute-start | bytes 331784 | tf_op jit(solution)/shard_map/ppermute | solution.py:441
  220.0 19.3 %collective-permute-start.12 = (bf16[2,512,768]{2,1,0:T(8,128)(2,1)}, bf16[2,512,768]{2,1,0:T(8,128)(2,1)}, u32[]{:S(2)}, u32[]{:S(2)}) collective-permute-start(bf16[2,512,768]{2,1,0:T(8,128)(2,1)} %get-tuple-element.69), channel_id=1, source_target_pairs={{0,8},{8,0},{16,24},{24,16},{1,9},{9,1},{17,25},{25,17},{2,10},{10... | collective-permute-start | bytes 4718600 | tf_op jit(solution)/shard_map/ppermute | solution.py:441
  222.3 5.0 %collective-permute-start.18 = (bf16[96,576]{1,0:T(8,128)(2,1)S(1)}, bf16[96,576]{1,0:T(8,128)(2,1)S(1)}, u32[]{:S(2)}, u32[]{:S(2)}) collective-permute-start(bf16[96,576]{1,0:T(8,128)(2,1)S(1)} %fusion.25), channel_id=1, source_target_pairs={{0,16},{8,24},{16,0},{24,8},{1,17},{9,25},{17,1},{25,9},{2,18},{10... | collective-permute-start | bytes 331784 | tf_op jit(solution)/shard_map/ppermute | solution.py:441
  226.5 9.4 %copy-start.3 = (bf16[8,128,768]{2,1,0:T(8,128)(2,1)}, bf16[8,128,768]{2,1,0:T(8,128)(2,1)S(1)}, u32[]{:S(2)}) copy-start(bf16[8,128,768]{2,1,0:T(8,128)(2,1)S(1)} %slice.121) | copy-start | bytes 4718596
  226.5 1.6 collective-permute-start.17
  227.3 1.8 collective-permute-start.19
  233.3 25.5 %collective-permute-start.21 = (bf16[8,144,384]{2,1,0:T(8,128)(2,1)}, bf16[8,144,384]{2,1,0:T(8,128)(2,1)}, u32[]{:S(2)}, u32[]{:S(2)}) collective-permute-start(bf16[8,144,384]{2,1,0:T(8,128)(2,1)} %add_convert_fusion), channel_id=1, source_target_pairs={{0,16},{8,24},{16,0},{24,8},{1,17},{9,25},{17,1},{25,9},{2,18},{10... | collective-permute-start | bytes 2654216 | tf_op jit(solution)/shard_map/ppermute | solution.py:441
  235.9 1.5 copy-start.5
  235.9 3.4 %copy-start.6 = (bf16[2,512,768]{2,1,0:T(8,128)(2,1)S(1)}, bf16[2,512,768]{2,1,0:T(8,128)(2,1)}, u32[]{:S(2)}) copy-start(bf16[2,512,768]{2,1,0:T(8,128)(2,1)} %get-tuple-element.68) | copy-start | bytes 4718596
  237.4 18.8 %collective-permute-start.25 = (bf16[2,2,128,768]{3,2,1,0:T(8,128)(2,1)}, bf16[2,2,128,768]{3,2,1,0:T(8,128)(2,1)}, u32[]{:S(2)}, u32[]{:S(2)}) collective-permute-start(bf16[2,2,128,768]{3,2,1,0:T(8,128)(2,1)} %fusion.15), channel_id=1, source_target_pairs={{0,1},{1,0},{2,3},{3,2},{4,5},{5,4},{6,7},{7,6},{8,9},{9,8},{10,11... | collective-permute-start | bytes 2359304 | tf_op jit(solution)/shard_map/ppermute | solution.py:441
  241.5 29.9 %collective-permute-start.13 = (bf16[512,768]{1,0:T(8,128)(2,1)}, bf16[512,768]{1,0:T(8,128)(2,1)}, u32[]{:S(2)}, u32[]{:S(2)}) collective-permute-start(bf16[512,768]{1,0:T(8,128)(2,1)} %fusion.14), channel_id=1, source_target_pairs={{0,16},{8,24},{16,0},{24,8},{1,17},{9,25},{17,1},{25,9},{2,18},{10... | collective-permute-start | bytes 2359304 | tf_op jit(solution)/shard_map/ppermute | solution.py:441
  244.4 11.7 %copy-start.4 = (bf16[8,128,768]{2,1,0:T(8,128)(2,1)S(1)}, bf16[8,128,768]{2,1,0:T(8,128)(2,1)}, u32[]{:S(2)}) copy-start(bf16[8,128,768]{2,1,0:T(8,128)(2,1)} %copy-done.3) | copy-start | bytes 4718596
  257.4 3.9 %copy-start.9 = (bf16[96,2304]{1,0:T(8,128)(2,1)S(1)}, bf16[96,2304]{1,0:T(8,128)(2,1)}, u32[]{:S(2)}) copy-start(bf16[96,2304]{1,0:T(8,128)(2,1)} %param.11) | copy-start | bytes 1327108
  257.4 3.9 %copy-start.10 = (bf16[96,2304]{1,0:T(8,128)(2,1)S(1)}, bf16[96,2304]{1,0:T(8,128)(2,1)}, u32[]{:S(2)}) copy-start(bf16[96,2304]{1,0:T(8,128)(2,1)} %concatenate.58) | copy-start | bytes 1327108
  257.4 16.0 %collective-permute-start.26 = (bf16[2,128,768]{2,1,0:T(8,128)(2,1)S(1)}, bf16[2,128,768]{2,1,0:T(8,128)(2,1)S(1)}, u32[]{:S(2)}, u32[]{:S(2)}) collective-permute-start(bf16[2,128,768]{2,1,0:T(8,128)(2,1)S(1)} %fusion.17), channel_id=1, source_target_pairs={{0,2},{1,3},{2,0},{3,1},{4,6},{5,7},{6,4},{7,5},{8,10},{9,11},{10,... | collective-permute-start | bytes 1179656 | tf_op jit(solution)/shard_map/ppermute | solution.py:441
  259.9 11.4 %copy-start.7 = (bf16[2,512,768]{2,1,0:T(8,128)(2,1)S(1)}, bf16[2,512,768]{2,1,0:T(8,128)(2,1)}, u32[]{:S(2)}) copy-start(bf16[2,512,768]{2,1,0:T(8,128)(2,1)} %get-tuple-element.68) | copy-start | bytes 4718596
  260.0 14.7 %collective-permute-start.22 = (bf16[2,2,144,384]{3,2,0,1:T(8,128)(2,1)S(1)}, bf16[2,2,144,384]{3,2,0,1:T(8,128)(2,1)S(1)}, u32[]{:S(2)}, u32[]{:S(2)}) collective-permute-start(bf16[2,2,144,384]{3,2,0,1:T(8,128)(2,1)S(1)} %copy.23), channel_id=1, source_target_pairs={{0,1},{1,0},{2,3},{3,2},{4,5},{5,4},{6,7},{7,6},{8,9},{9,8},{10,11... | collective-permute-start | bytes 1327112 | tf_op jit(solution)/shard_map/ppermute | solution.py:441
  274.6 11.0 %collective-permute-start.27 = (bf16[128,768]{1,0:T(8,128)(2,1)S(1)}, bf16[128,768]{1,0:T(8,128)(2,1)S(1)}, u32[]{:S(2)}, u32[]{:S(2)}) collective-permute-start(bf16[128,768]{1,0:T(8,128)(2,1)S(1)} %fusion.22), channel_id=1, source_target_pairs={{0,4},{1,5},{2,6},{3,7},{4,0},{5,1},{6,2},{7,3},{8,12},{9,13},{10,... | collective-permute-start | bytes 589832 | tf_op jit(solution)/shard_map/ppermute | solution.py:441
  275.7 12.1 %collective-permute-start.23 = (bf16[2,144,384]{2,1,0:T(8,128)(2,1)S(1)}, bf16[2,144,384]{2,1,0:T(8,128)(2,1)S(1)}, u32[]{:S(2)}, u32[]{:S(2)}) collective-permute-start(bf16[2,144,384]{2,1,0:T(8,128)(2,1)S(1)} %fusion.21), channel_id=1, source_target_pairs={{0,2},{1,3},{2,0},{3,1},{4,6},{5,7},{6,4},{7,5},{8,10},{9,11},{10,... | collective-permute-start | bytes 663560 | tf_op jit(solution)/shard_map/ppermute | solution.py:441
  277.1 28.3 %copy-start.12 = (f32[512,768]{1,0:T(8,128)S(1)}, f32[512,768]{1,0:T(8,128)}, u32[]{:S(2)}) copy-start(f32[512,768]{1,0:T(8,128)} %get-tuple-element.51) | copy-start | bytes 4718596
  286.7 3.5 %collective-permute-start.28 = (bf16[128,384]{1,0:T(8,128)(2,1)S(1)}, bf16[128,384]{1,0:T(8,128)(2,1)S(1)}, u32[]{:S(2)}, u32[]{:S(2)}) collective-permute-start(bf16[128,384]{1,0:T(8,128)(2,1)S(1)} %fusion.32), channel_id=1, source_target_pairs={{0,16},{8,24},{16,0},{24,8},{1,17},{9,25},{17,1},{25,9},{2,18},{10... | collective-permute-start | bytes 294920 | tf_op jit(solution)/shard_map/ppermute | solution.py:441
  288.8 7.9 %collective-permute-start.24 = (bf16[144,384]{1,0:T(8,128)(2,1)S(1)}, bf16[144,384]{1,0:T(8,128)(2,1)S(1)}, u32[]{:S(2)}, u32[]{:S(2)}) collective-permute-start(bf16[144,384]{1,0:T(8,128)(2,1)S(1)} %fusion.28), channel_id=1, source_target_pairs={{0,4},{1,5},{2,6},{3,7},{4,0},{5,1},{6,2},{7,3},{8,12},{9,13},{10,... | collective-permute-start | bytes 331784 | tf_op jit(solution)/shard_map/ppermute | solution.py:441
  297.7 6.1 %collective-permute-start.30 = (bf16[272,384]{1,0:T(8,128)(2,1)S(1)}, bf16[272,384]{1,0:T(8,128)(2,1)S(1)}, u32[]{:S(2)}, u32[]{:S(2)}) collective-permute-start(bf16[272,384]{1,0:T(8,128)(2,1)S(1)} %pad_maximum_fusion.9), channel_id=1, source_target_pairs={{0,16},{8,24},{16,0},{24,8},{1,17},{9,25},{17,1},{25,9},{2,18},{10... | collective-permute-start | bytes 626696 | tf_op jit(solution)/shard_map/ppermute | solution.py:441
  298.1 10.3 %collective-permute-start.29 = (bf16[272,384]{1,0:T(8,128)(2,1)S(1)}, bf16[272,384]{1,0:T(8,128)(2,1)S(1)}, u32[]{:S(2)}, u32[]{:S(2)}) collective-permute-start(bf16[272,384]{1,0:T(8,128)(2,1)S(1)} %pad_maximum_fusion.9), channel_id=1, source_target_pairs={{0,8},{8,0},{16,24},{24,16},{1,9},{9,1},{17,25},{25,17},{2,10},{10... | collective-permute-start | bytes 626696 | tf_op jit(solution)/shard_map/ppermute | solution.py:441
  303.8 4.5 %collective-permute-start.31 = (bf16[272,384]{1,0:T(8,128)(2,1)S(1)}, bf16[272,384]{1,0:T(8,128)(2,1)S(1)}, u32[]{:S(2)}, u32[]{:S(2)}) collective-permute-start(bf16[272,384]{1,0:T(8,128)(2,1)S(1)} %collective-permute-done.30), channel_id=1, source_target_pairs={{0,8},{8,0},{16,24},{24,16},{1,9},{9,1},{17,25},{25,17},{2,10},{10... | collective-permute-start | bytes 626696 | tf_op jit(solution)/shard_map/ppermute | solution.py:441
  308.6 1.6 copy-start.11
Sparse Core Ops, SparseCore 0:
  11.5 82.3 all-gather.1
